TPU v7x, 128 devices: a whole 4x4x4 slice. The times are simulated.
128 devices in a mesh: replica: 8 (over z, y_lo), tensor: 16 (over x, y_hi, core).
Axes of the slice: x: 4, y: 4 (y_hi: 2, y_lo: 2; y = y_hi * 2 + y_lo), z: 4, core: 2. Of those that a mesh axis runs over, the one named last changes fastest.
Arguments:
- hidden_in: bfloat16 [2, 128, 8192], P(None, 'replica'), may hold values from -6 to 6
- norm_gain: float32 [8192], replicated, may hold values from 0.1 to 1.9
- qkv_buckets: bfloat16 [256, 32, 10240], P(('replica', 'tensor')), may hold values from -0.0625 to 0.0625
- bucket_slot: int32 [256], replicated, may hold values from 0 to 255, each once
- kv_cache: bfloat16 [128, 16384, 256], P('replica', 'tensor')
- cache_len: int32 [128], P('replica'), may hold values from 1 to 2048, as said below
Outputs:
- context: bfloat16 [2, 128, 8192], P(None, 'replica', 'tensor')
- served_weight: bfloat16 [16, 8192, 768], P('tensor')
Inputs may be any that keep to these rules, and one draw needn't show every extreme that they name: `cache_len`: each row has at least one valid cached position, and some row holds all 2048.
All inputs are finite; a program needn't handle non-finite values.
Results may differ from a plain program's by a relative error of at most 0.015.
The roundings to bfloat16 on the way count: a program that leaves them out, or rounds other values in their place, can miss the bound.
Values may be sent and summed in bfloat16 or wider, within the bound.
A program may use at most 128 MiB of HBM per device.

v0:
```python
import jax
import jax.numpy as jnp
from jax import lax
from jax.sharding import PartitionSpec as P

QH = 64
KVH = 8
HD = 128


rope_base = 500000.0
norm_eps = 1e-05
masked_score = -1e30


def from_partner(block, axis, apart):
    count = lax.axis_size(axis)
    route = []
    for low in range(count):
        high = low | 1 << apart
        if high != low and high < count:
            route += [(low, high), (high, low)]
    return lax.ppermute(block, axis, route)


def rotate(vectors, positions):
    half_dim = HD // 2
    freqs = rope_base ** (-2.0 * jnp.arange(half_dim, dtype=jnp.float32) / HD)
    angles = positions.astype(jnp.float32)[..., None] * freqs
    cosine = jnp.cos(angles)
    sine = jnp.sin(angles)
    first = vectors[..., :half_dim]
    second = vectors[..., half_dim:]
    return jnp.concatenate(
        [first * cosine - second * sine, second * cosine + first * sine], axis=-1
    )


def partial_attention(queries, cache_block, lengths, pos_offset):
    scale_factor = HD ** (-0.5)
    pos_count = cache_block.shape[1]
    scores = (
        jnp.einsum(
            "sbhd,bpd->sbhp", queries, cache_block[..., :HD], preferred_element_type=jnp.float32
        )
        * scale_factor
    )
    valid = (pos_offset + jnp.arange(pos_count, dtype=jnp.int32))[None, :] < lengths[:, None]
    valid = valid[None, :, None, :]
    masked = jnp.where(valid, scores, masked_score)
    peaks = jnp.max(masked, axis=-1)
    shifted = jnp.where(valid, masked - peaks[..., None], masked_score)
    probs = jnp.exp(shifted).astype(jnp.bfloat16)
    totals = jnp.sum(probs.astype(jnp.float32), axis=-1)
    weighted = jnp.einsum(
        "sbhp,bpd->sbhd", probs, cache_block[..., HD:], preferred_element_type=jnp.float32
    )
    return (peaks, totals, weighted)


def combine(current, incoming):
    peaks, totals, weighted = current
    peaks_in, totals_in, weighted_in = incoming
    merged = jnp.maximum(peaks, peaks_in)
    factor_own = jnp.exp(peaks - merged)
    factor_in = jnp.exp(peaks_in - merged)
    return (
        merged,
        totals * factor_own + totals_in * factor_in,
        weighted * factor_own[..., None] + weighted_in * factor_in[..., None],
    )


def on_device(hidden_in, norm_gain, qkv_buckets, bucket_slot, kv_cache, cache_len):
    tensor_count = lax.axis_size("tensor")
    replica_count = lax.axis_size("replica")
    query_width = QH * HD
    kv_width = KVH * HD
    per_head = tensor_count // KVH
    query_cols = query_width // tensor_count
    local_heads = query_cols // HD
    bucket_local, bucket_rows, joined_width = qkv_buckets.shape
    steps_count, row_count, model_width = hidden_in.shape
    bucket_count = model_width // bucket_rows
    q_part = qkv_buckets[:, :, :query_width].reshape(
        bucket_local, bucket_rows, tensor_count, query_cols
    )
    kv_shape = (bucket_local, bucket_rows, KVH, per_head, HD)
    k_part = jnp.broadcast_to(
        qkv_buckets[:, :, query_width : query_width + kv_width].reshape(
            bucket_local, bucket_rows, KVH, 1, HD
        ),
        kv_shape,
    )
    k_part = k_part.reshape(bucket_local, bucket_rows, tensor_count, HD)
    v_part = jnp.broadcast_to(
        qkv_buckets[:, :, query_width + kv_width :].reshape(bucket_local, bucket_rows, KVH, 1, HD),
        kv_shape,
    )
    v_part = v_part.reshape(bucket_local, bucket_rows, tensor_count, HD)
    packed = jnp.transpose(jnp.concatenate([q_part, k_part, v_part], axis=3), (2, 0, 1, 3))
    column_count = packed.shape[-1]
    inputs = hidden_in.astype(jnp.float32)
    normed = (
        inputs * lax.rsqrt(jnp.mean(inputs * inputs, axis=-1, keepdims=True) + norm_eps) * norm_gain
    )
    normed = normed.astype(jnp.bfloat16)
    normed_rows = normed.reshape(steps_count * row_count, model_width)
    outgoing = jnp.broadcast_to(packed[None], (replica_count,) + packed.shape)
    outgoing = outgoing.reshape((replica_count * tensor_count,) + packed.shape[1:])
    arrived = lax.all_to_all(
        outgoing, ("replica", "tensor"), split_axis=0, concat_axis=0, tiled=True
    )
    arrived = arrived.reshape(bucket_count, bucket_rows, column_count)
    served = jnp.take(arrived, bucket_slot, axis=0).reshape(model_width, column_count)
    projected = jnp.dot(normed_rows, served, preferred_element_type=jnp.float32)
    projected = projected.reshape(steps_count, row_count, column_count)
    positions = cache_len[None, :] + jnp.arange(steps_count, dtype=jnp.int32)[:, None]
    queries = rotate(
        projected[..., :query_cols].reshape(steps_count, row_count, local_heads, HD),
        positions[..., None],
    ).astype(jnp.bfloat16)
    keys_new = rotate(projected[..., query_cols : query_cols + HD], positions).astype(jnp.bfloat16)
    values_new = projected[..., query_cols + HD :].astype(jnp.bfloat16)
    tensor_index = lax.axis_index("tensor")
    member = tensor_index % per_head
    bit_total = per_head.bit_length() - 1
    group_block = queries
    bit_index = 0
    partner = from_partner(group_block, "tensor", bit_index)
    upper = tensor_index // (1 << bit_index) % 2
    group_block = jnp.where(
        upper == 1,
        jnp.concatenate([partner, group_block], axis=2),
        jnp.concatenate([group_block, partner], axis=2),
    )
    pos_offset = member * kv_cache.shape[1]
    attention = partial_attention(group_block, kv_cache, cache_len, pos_offset)
    bit_index = 0
    incoming = from_partner((attention[0], attention[1], attention[2]), "tensor", bit_index)
    attention = combine(attention, incoming)
    head_start = member * local_heads
    peaks = lax.dynamic_slice_in_dim(attention[0], head_start, local_heads, 2)
    totals = lax.dynamic_slice_in_dim(attention[1], head_start, local_heads, 2)
    weighted = lax.dynamic_slice_in_dim(attention[2], head_start, local_heads, 2)
    scale_factor = HD ** (-0.5)
    fresh = (
        jnp.einsum("sbhd,tbd->sbht", queries, keys_new, preferred_element_type=jnp.float32)
        * scale_factor
    )
    causal = (jnp.arange(steps_count)[None, :] <= jnp.arange(steps_count)[:, None])[
        :, None, None, :
    ]
    fresh = jnp.where(causal, fresh, masked_score)
    merged = jnp.maximum(peaks, jnp.max(fresh, axis=-1))
    carried = jnp.exp(peaks - merged)
    fresh_probs = jnp.where(causal, jnp.exp(fresh - merged[..., None]), 0.0).astype(jnp.bfloat16)
    totals = totals * carried + jnp.sum(fresh_probs.astype(jnp.float32), axis=-1)
    weighted = weighted * carried[..., None] + jnp.einsum(
        "sbht,tbd->sbhd", fresh_probs, values_new, preferred_element_type=jnp.float32
    )
    context = (
        (weighted / totals[..., None])
        .astype(jnp.bfloat16)
        .reshape(steps_count, row_count, query_cols)
    )
    return (context, served[None])


def solution(mesh):
    in_specs = (
        P(None, "replica", None),
        P(),
        P(("replica", "tensor"), None, None),
        P(),
        P("replica", "tensor", None),
        P("replica"),
    )
    out_specs = (P(None, "replica", "tensor"), P("tensor", None, None))
    return jax.shard_map(
        on_device, mesh=mesh, in_specs=in_specs, out_specs=out_specs, check_vma=False
    )
```

profile of v0, /device:TPU:67, one launch (start us, length us, event | category | flops | bytes accessed | tf_op | source)
XLA Modules:
  0.0 239.9 jit_solution(16300858778818574562)
XLA Ops:
  0.6 1.0 fusion.53
  1.6 1.3 slice.37
  3.0 0.4 copy.34
  3.3 0.2 broadcast_in_dim.109
  3.5 0.2 broadcast_in_dim.107
  3.7 0.1 maximum_bitcast_fusion
  3.8 0.5 copy.16
  4.3 6.4 %broadcast_in_dim.110 = bf16[8,16,2,32,768]{4,3,2,1,0:T(8,128)(2,1)} broadcast(bf16[16,2,32,768]{3,2,1,0:T(8,128)(2,1)S(1)} %copy.16), dimensions={1,2,3,4} | broadcast | bytes 14155776 | tf_op jit(solution)/shard_map/broadcast_in_dim | solution.py:109
  10.7 0.0 copy-start.2
  10.7 0.0 copy-start
  10.7 0.0 copy-start.3
  10.7 10.7 %all-to-all-start = ((bf16[128,2,32,768]{3,2,1,0:T(8,128)(2,1)}), bf16[128,2,32,768]{3,2,1,0:T(8,128)(2,1)}, u32[]{:S(2)}, u32[]{:S(2)}) async-start(bf16[128,2,32,768]{3,2,1,0:T(8,128)(2,1)} %bitcast.74), calls=%async_computation | async-start | bytes 25165824 | tf_op jit(solution)/shard_map/all_to_all | solution.py:111
  21.4 0.0 copy-done.2
  21.4 0.1 broadcast_in_dim.103
  21.6 0.1 broadcast_in_dim.104
  21.8 0.0 copy-done
  21.8 0.2 fusion.22
  22.0 0.0 copy-done.3
  22.0 0.1 broadcast_compare_fusion
  22.1 167.9 %all-to-all-done = bf16[128,2,32,768]{3,2,1,0:T(8,128)(2,1)} async-done(((bf16[128,2,32,768]{3,2,1,0:T(8,128)(2,1)}), bf16[128,2,32,768]{3,2,1,0:T(8,128)(2,1)}, u32[]{:S(2)}, u32[]{:S(2)}) %all-to-all-start) | async-done | bytes 12582944 | tf_op jit(solution)/shard_map/all_to_all | solution.py:111
  190.0 15.4 %gather_fusion = bf16[256,32,768]{2,1,0:T(8,128)(2,1)} fusion(bf16[256,32,768]{2,1,0:T(8,128)(2,1)} %bitcast.4, s32[1024]{0:T(1024)S(1)} %pad_clamp_fusion), kind=kCustom, calls=%fused_computation | custom fusion | bytes 25166848 | tf_op jit(solution)/shard_map/jit(_take)/gather | solution.py:115
  205.4 0.0 copy-start.1
  205.4 8.0 %bitcast_select_fusion.1 = bf16[8192,768]{1,0:T(8,128)(2,1)S(1)} fusion(bf16[256,32,768]{2,1,0:T(8,128)(2,1)} %gather_fusion, pred[8192]{0:T(1024)(128)(4,1)S(1)} %broadcast_in_dim.104), kind=kLoop, calls=%fused_computation.4 | loop fusion | flops 6291456 | bytes 25174016 | tf_op jit(solution)/shard_map/jit(_take)/select_n | solution.py:115
  213.4 0.0 copy-done.1
  213.4 2.3 fusion
  215.7 0.1 fusion.54
  215.8 0.1 subtract_convert_fusion.1
  216.1 0.1 pad_maximum_fusion
  216.2 1.4 collective-permute-start
  217.6 12.0 %bitcast_select_fusion = bf16[1,8192,768]{2,1,0:T(8,128)(2,1)} fusion(pred[8192]{0:T(1024)(128)(4,1)S(1)} %broadcast_in_dim.104, bf16[1,8192,768]{2,1,0:T(8,128)(2,1)} %bitcast.73), kind=kLoop, calls=%fused_computation.1 | loop fusion | flops 6291456 | bytes 25174016 | tf_op jit(solution)/shard_map/jit(_take)/select_n | solution.py:115
  229.6 0.1 maximum_bitcast_fusion.1
  229.6 0.4 fusion.56
  230.1 0.0 collective-permute-done
  230.1 3.5 %fusion.55 = (f32[2,16,8]{2,0,1:T(2,128)S(1)}, f32[2,16,8,1024]{3,2,0,1:T(8,128)S(1)}) fusion(bf16[16,1024,256]{2,1,0:T(8,128)(2,1)} %param.10, bf16[2,16,4,64]{3,2,0,1:T(4,128)(2,1)S(1)} %get-tuple-element.15, bf16[2,16,4,64]{3,2,0,1:T(4,128)(2,1)S(1)} %get-tuple-element.14, bf16[2,16,4,128]{3,2,0,1:T(4,128)(2,1)S(1)} %collective-permute-done, ...), kind=kOutput, calls=%fused_computation.85 | convolution fusion | flops 68321024 | bytes 5325825 | tf_op jit(solution)/shard_map/sbhd,bpd->sbhp/dot_general | solution.py:43
  233.6 0.1 collective-permute-start.1
  233.7 3.0 %fusion.17 = f32[2,16,8,128]{3,2,0,1:T(8,128)S(1)} fusion(bf16[16,1024,256]{2,1,0:T(8,128)(2,1)} %param.10, f32[2,16,8,1024]{3,2,0,1:T(8,128)S(1)} %get-tuple-element.25, f32[2,16,8]{2,0,1:T(2,128)S(1)} %get-tuple-element.24, pred[16,1024]{1,0:T(8,128)(4,1)S(1)} %broadcast_compare_fusion), kind=kOutput, calls=%fused_computation.17 | convolution fusion | flops 67895296 | bytes 5391360 | tf_op jit(solution)/shard_map/sbhp,bpd->sbhd/dot_general | solution.py:55
  236.7 0.4 convert_reduce_fusion
  237.1 0.6 collective-permute-start.2
  237.7 0.1 collective-permute-start.3
  237.8 0.0 collective-permute-done.1
  237.8 0.1 dynamic-slice_maximum_fusion
  237.9 0.1 convert_reduce_fusion.1
  238.0 0.8 collective-permute-done.3
  238.9 0.2 fusion.45
  239.0 0.0 collective-permute-done.2
  239.0 0.3 fusion.42
  239.3 0.6 copy.23
  (19 shorter events, 0.2 us)
Async XLA Ops:
  10.7 10.8 %copy-start.2 = (s32[256]{0:T(256)S(1)}, s32[256]{0:T(256)}, u32[]{:S(2)}) copy-start(s32[256]{0:T(256)} %param.9) | copy-start | bytes 3076
  10.7 11.1 %copy-start = (bf16[2,16,8192]{2,1,0:T(8,128)(2,1)S(1)}, bf16[2,16,8192]{2,1,0:T(8,128)(2,1)}, u32[]{:S(2)}) copy-start(bf16[2,16,8192]{2,1,0:T(8,128)(2,1)} %param.6) | copy-start | bytes 1572868
  10.7 11.3 %copy-start.3 = (s32[16]{0:T(128)S(1)}, s32[16]{0:T(128)}, u32[]{:S(2)}) copy-start(s32[16]{0:T(128)} %param.11) | copy-start | bytes 196
  10.7 179.3 %all-to-all-start = ((bf16[128,2,32,768]{3,2,1,0:T(8,128)(2,1)}), bf16[128,2,32,768]{3,2,1,0:T(8,128)(2,1)}, u32[]{:S(2)}, u32[]{:S(2)}) async-start(bf16[128,2,32,768]{3,2,1,0:T(8,128)(2,1)} %bitcast.74), calls=%async_computation | async-start | bytes 25165824 | tf_op jit(solution)/shard_map/all_to_all | solution.py:111
  205.4 8.0 %copy-start.1 = (f32[8192]{0:T(1024)S(1)}, f32[8192]{0:T(1024)}, u32[]{:S(2)}) copy-start(f32[8192]{0:T(1024)} %param.7) | copy-start | bytes 98308
  216.2 13.9 %collective-permute-start = (bf16[2,16,4,128]{3,2,0,1:T(4,128)(2,1)S(1)}, bf16[2,16,4,128]{3,2,0,1:T(4,128)(2,1)S(1)}, u32[]{:S(2)}, u32[]{:S(2)}) collective-permute-start(bf16[2,16,4,128]{3,2,0,1:T(4,128)(2,1)S(1)} %pad_maximum_fusion), channel_id=1, source_target_pairs={{0,1},{1,0},{2,3},{3,2},{4,5},{5,4},{6,7},{7,6},{8,9},{9,8},{10,11... | collective-permute-start | bytes 98312 | tf_op jit(solution)/shard_map/ppermute | solution.py:23
  233.6 4.1 %collective-permute-start.1 = (f32[2,16,8]{2,0,1:T(2,128)S(1)}, f32[2,16,8]{2,0,1:T(2,128)S(1)}, u32[]{:S(2)}, u32[]{:S(2)}) collective-permute-start(f32[2,16,8]{2,0,1:T(2,128)S(1)} %get-tuple-element.24), channel_id=1, source_target_pairs={{0,1},{1,0},{2,3},{3,2},{4,5},{5,4},{6,7},{7,6},{8,9},{9,8},{10,11... | collective-permute-start | bytes 3080 | tf_op jit(solution)/shard_map/ppermute | solution.py:23
  237.1 1.9 collective-permute-start.2
  237.7 1.2 collective-permute-start.3
where the time goes:
time: 240 us
  waiting for transfers between devices  169 us (70%)
  local copies, waits for them, and re-layouts  26.2 us (11%)
  other arithmetic  21.5 us (9%)
  starting transfers between devices  12.9 us (5%)
  matrix products  9.51 us (4%)
    all_to_all x1, waiting for transfers between devices, on_device(): lax.all_to_all(outgoing, ('replica', 'tensor'), split_axis=0, concat_axis...  168 us
    select_n x3, other arithmetic, on_device(): jnp.take(arrived, bucket_slot, axis=0).reshape(model_width, column_count)  19.9 us
    gather x1, local copies, waits for them, and re-layouts, on_device(): jnp.take(arrived, bucket_slot, axis=0).reshape(model_width, column_count)  15.4 us
    all_to_all x1, starting transfers between devices, on_device(): lax.all_to_all(outgoing, ('replica', 'tensor'), split_axis=0, concat_axis...  10.7 us
    broadcast_in_dim x1, local copies, waits for them, and re-layouts, on_device(): outgoing = jnp.broadcast_to(packed[None], (replica_count,) + packed.shape)  6.38 us
  transfers between devices with their start and end apart: 5, of which 2 were waited for; matrix products, arithmetic and copies ran while one was open for 7% of the time, Pallas kernels for 0%

commit v1 on v0

v1 whole, which is shorter than its diff:
```python
import functools
import heapq
import itertools

import jax
import jax.numpy as jnp
import numpy as np
from jax import lax
from jax.experimental import pallas as pl
from jax.experimental.pallas import tpu as pltpu
from jax.sharding import PartitionSpec as P

QH = 64
KVH = 8
HD = 128
D = 8192
LEN = 2048
STEPS = 2
BROWS = 32
NB = 256
N_TENSOR = 16
N_REPLICA = 8
ROWS = 16
M = STEPS * ROWS
QC = 512
OWN = QC + HD
COLS = QC + 2 * HD
HEADS = QC // HD
HALF = LEN // 2

rope_base = 500000.0
norm_eps = 1e-05
masked_score = -1e30

MESH = pl.DeviceIdType.MESH

UNITS = ((0, 0), (1, 0), (3, 0), (0, 1), (1, 1), (3, 1), (2, 0), (2, 1))
ITEMS = ((0, 0, 2), (0, 2, 2)) + tuple((u, 0, 4) for u in range(1, 8))
PAIR_FIRST = frozenset((0, 2, 4, 5, 7))


def event_order():
    per_slot, hop = 0.87, 0.8
    entry = (0.8, 1.2, 4.0, 4.0, 4.5, 7.5, 8.5, 13.0, 14.0)
    links = ("pair", "up", "down")
    free = dict.fromkeys(links, 0.0)
    queue = {link: [] for link in links}
    count = itertools.count()
    events = [(entry[i], next(count), ("entry", i)) for i in range(len(ITEMS))]
    heapq.heapify(events)
    order = []
    while events:
        now, _, event = heapq.heappop(events)
        if event is not None:
            order.append(event)
            for link, arrival, slots in forwards(event):
                queue[link].append((arrival, slots))
        for link in links:
            if queue[link] and free[link] <= now + 1e-9:
                arrival, slots = queue[link].pop(0)
                free[link] = now + slots * per_slot
                heapq.heappush(events, (free[link] + hop, next(count), arrival))
                heapq.heappush(events, (free[link], next(count), None))
    return order


def forwards(event):
    kind, item = event[0], event[1]
    slots = ITEMS[item][2]
    sends = []
    if kind == "entry":
        sends += [("pair", ("pair", item), slots)]
        sends += [("up", ("up1", item, 0), slots), ("down", ("down1", item, 0), slots)]
    elif kind == "pair" and item in PAIR_FIRST:
        sends += [("up", ("up1", item, 1), slots), ("down", ("down1", item, 1), slots)]
    elif kind in ("up1", "down1"):
        link = kind[:-1]
        sends += [(link, (link + "2", item, event[2]), slots // 2)]
        if item not in PAIR_FIRST:
            sends += [("pair", ("late", item, kind), slots)]
    elif kind in ("up2", "down2") and item not in PAIR_FIRST:
        sends += [("pair", ("late", item, kind), slots // 2)]
    return sends


EVENTS = event_order()
PLACE = {event: i for i, event in enumerate(EVENTS)}


def gather_kernel(
    hid_hbm,
    gain_hbm,
    buckets,
    slot_hbm,
    cache,
    freq_ref,
    len_ref,
    arr,
    proj,
    cos_ref,
    sin_ref,
    cache_other,
    hid,
    gain,
    slot_row,
    inv_row,
    inv,
    turned,
    lhs,
    local_sem,
    prep_sem,
    own_sem,
    recv_sem,
    entry_sem,
    link_sem,
    stage_sem,
    kv_send,
    kv_recv,
    cache_send,
    cache_recv,
):
    r = lax.axis_index("replica")
    t = lax.axis_index("tensor")
    z, p = r // 2, r % 2
    x, h, c = t // 4, (t // 2) % 2, t % 2
    other_core = (r, x * 4 + h * 2 + (1 - c))
    target = {
        "pair": (z * 2 + (1 - p), t),
        "up": (((z + 1) % 4) * 2 + p, t),
        "down": (((z + 3) % 4) * 2 + p, t),
    }
    own_col = pl.multiple_of(QC + HD * c, HD)
    other_col = pl.multiple_of(QC + HD * (1 - c), HD)

    prep = [
        pltpu.make_async_copy(hid_hbm, hid, prep_sem.at[0]),
        pltpu.make_async_copy(gain_hbm, gain, prep_sem.at[1]),
        pltpu.make_async_copy(slot_hbm, slot_row, prep_sem.at[2]),
    ]
    for copy in prep:
        copy.start()

    def chip(dx, dh, core):
        return (z * 2 + (p + dh) % 2, ((x + dx) % 4) * 4 + ((h + dh) % 2) * 2 + core)

    barrier = pltpu.get_barrier_semaphore()
    peers = [other_core] + list(target.values())
    peers += [chip(dx, dh, core) for dx, dh in UNITS[1:] for core in range(2)]
    for peer in peers:
        pl.semaphore_signal(barrier, inc=1, device_id=peer, device_id_type=MESH)
    pl.semaphore_wait(barrier, len(peers))

    mine = (r * N_TENSOR + t) * 2

    def parts(base, slots):
        rows = pl.ds(base, slots)
        return arr.at[rows, :, pl.ds(0, QC)], arr.at[rows, :, pl.ds(own_col, HD)]

    def bucket_parts(x_to, h_to, core):
        group = x_to * 2 + h_to
        query = pl.multiple_of((group * 2 + core) * QC, QC)
        key = pl.multiple_of(QH * HD + core * (KVH * HD) + group * HD, HD)
        return buckets.at[:, :, pl.ds(query, QC)], buckets.at[:, :, pl.ds(key, HD)]

    def send_unit(unit):
        dx, dh = UNITS[unit]
        x_to, h_to, p_to = (x + 4 - dx) % 4, (h + dh) % 2, (p + dh) % 2
        for core in range(2):
            dst = (z * 2 + p_to, x_to * 4 + h_to * 2 + core)
            source = bucket_parts(x_to, h_to, core)
            cols = (pl.ds(0, QC), pl.ds(QC + HD * core, HD))
            for src, col in zip(source, cols):
                pltpu.make_async_remote_copy(
                    src_ref=src,
                    dst_ref=arr.at[pl.ds(mine, 2), :, col],
                    send_sem=stage_sem.at[0],
                    recv_sem=entry_sem.at[2 * unit + c],
                    device_id=dst,
                    device_id_type=MESH,
                ).start()

    def wait_bytes(slots, sem):
        ref = arr.at[pl.ds(0, slots), :, pl.ds(0, OWN)]
        pltpu.make_async_copy(ref, ref, sem).wait()

    own_copies = []
    for src, dst in zip(bucket_parts(x, h, c), parts(mine, 2)):
        copy = pltpu.make_async_copy(src, dst, own_sem.at[len(own_copies)])
        copy.start()
        own_copies.append(copy)
    for src, col in zip(bucket_parts(x, h, 1 - c), (pl.ds(0, QC), pl.ds(other_col, HD))):
        pltpu.make_async_remote_copy(
            src_ref=src,
            dst_ref=arr.at[pl.ds(mine, 2), :, col],
            send_sem=stage_sem.at[0],
            recv_sem=entry_sem.at[0],
            device_id=other_core,
            device_id_type=MESH,
        ).start()
    for unit in (1, 2, 3):
        send_unit(unit)

    def unit_base(unit, z_of, p_of):
        dx, dh = UNITS[unit]
        source = z_of * 2 + (p_of + dh) % 2
        return source * 32 + ((x + dx) % 4) * 8 + ((h + dh) % 2) * 4

    up_z, down_z, far_z = (z + 3) % 4, (z + 1) % 4, (z + 2) % 4

    def place(event):
        kind, item = event[0], event[1]
        unit, first, slots = ITEMS[item]
        if kind == "entry":
            z_of, p_of = z, p
        elif kind == "pair":
            z_of, p_of = z, 1 - p
        else:
            way = event[2] if kind == "late" else kind
            z_of = {"up1": up_z, "down1": down_z, "up2": far_z, "down2": far_z}[way]
            if kind == "late":
                p_of = 1 - p
            else:
                p_of = (p + event[2]) % 2
            if way in ("up2", "down2"):
                slots = slots // 2
                if way == "down2":
                    first = first + slots
        base = unit_base(unit, z_of, p_of)
        if unit == 0:
            own_half = 2 * c if item == 0 else 2 * (1 - c)
            base = base + own_half + (first - ITEMS[item][1])
        else:
            base = base + first
        return base, slots

    def wait_for(event):
        if event == ("entry", 0):
            for copy in own_copies:
                copy.wait()
        elif event == ("entry", 1):
            wait_bytes(2, entry_sem.at[0])
        elif event[0] == "entry":
            unit = ITEMS[event[1]][0]
            for core in range(2):
                wait_bytes(2, entry_sem.at[2 * unit + core])
        else:
            wait_bytes(place(event)[1], recv_sem.at[PLACE[event]])

    sent = {"pair": 0, "up": 0, "down": 0}
    link_index = {"pair": 0, "up": 1, "down": 2}

    def forward(event):
        base, _ = place(event)
        for link, arrival, slots in forwards(event):
            start = base
            if arrival[0] == "down2":
                start = base + slots
            for ref in parts(start, slots):
                pltpu.make_async_remote_copy(
                    src_ref=ref,
                    dst_ref=ref,
                    send_sem=link_sem.at[link_index[link]],
                    recv_sem=recv_sem.at[PLACE[arrival]],
                    device_id=target[link],
                    device_id_type=MESH,
                ).start()
            sent[link] += slots

    def share(event):
        base, slots = place(event)
        ref = arr.at[pl.ds(base, slots), :, pl.ds(own_col, HD)]
        pltpu.make_async_remote_copy(
            src_ref=ref,
            dst_ref=ref,
            send_sem=kv_send.at[0],
            recv_sem=kv_recv.at[PLACE[event]],
            device_id=other_core,
            device_id_type=MESH,
        ).start()

    def shared_wait(event):
        _, slots = place(event)
        ref = arr.at[pl.ds(0, slots), :, pl.ds(QC, HD)]
        pltpu.make_async_copy(ref, ref, kv_recv.at[PLACE[event]]).wait()

    def send_cache(row):
        pltpu.make_async_remote_copy(
            src_ref=cache.at[pl.ds(row, 1)],
            dst_ref=cache_other.at[pl.ds(row, 1)],
            send_sem=cache_send.at[0],
            recv_sem=cache_recv.at[0],
            device_id=other_core,
            device_id_type=MESH,
        ).start()

    def prepare():
        for copy in prep:
            copy.wait()
        slots = jnp.broadcast_to(slot_row[...], (NB, NB))
        by_bucket = jnp.transpose(slots)
        hit = by_bucket == lax.broadcasted_iota(jnp.int32, (NB, NB), 1)
        bucket = lax.broadcasted_iota(jnp.int32, (NB, NB), 0)
        inv_row[...] = jnp.max(jnp.where(hit, bucket, 0), axis=0, keepdims=True)
        move = pltpu.make_async_copy(inv_row, inv, prep_sem.at[3])
        move.start()

        def squares(j, total):
            part = hid[:, pl.ds(pl.multiple_of(j * 512, 512), 512)].astype(jnp.float32)
            return total + jnp.sum(part * part, axis=-1, keepdims=True)

        total = lax.fori_loop(0, D // 512, squares, jnp.zeros((M, 1), jnp.float32))
        factor = lax.rsqrt(total * (1.0 / D) + norm_eps)

        def turn(j, carry):
            cols = pl.ds(pl.multiple_of(j * 128, 128), 128)
            part = hid[:, cols].astype(jnp.float32) * factor * gain[:, cols]
            part = part.astype(jnp.bfloat16).astype(jnp.float32)
            part = jnp.transpose(part).astype(jnp.bfloat16)
            turned[pl.ds(j * 4, 4)] = part.reshape(4, BROWS, M)
            return carry

        lax.fori_loop(0, D // 128, turn, 0)
        move.wait()

        def pick(j, carry):
            rows = [turned[inv[0, j * 4 + i]] for i in range(4)]
            part = jnp.concatenate(rows, axis=0).astype(jnp.float32)
            lhs[j] = jnp.transpose(part).astype(jnp.bfloat16)
            return carry

        lax.fori_loop(0, NB // 4, pick, 0)

        row = lax.broadcasted_iota(jnp.int32, (M, HD), 0)
        position = jnp.zeros((M, HD), jnp.int32)
        for b in range(ROWS):
            for s in range(STEPS):
                position = jnp.where(row == s * ROWS + b, len_ref[b] + s, position)
        angle = position.astype(jnp.float32) * freq_ref[...]
        lane = lax.broadcasted_iota(jnp.int32, (M, HD), 1)
        cos_ref[...] = jnp.cos(angle)
        sine = jnp.sin(angle)
        sin_ref[...] = jnp.where(lane < HD // 2, -sine, sine)
        proj[...] = jnp.zeros_like(proj)

    def multiply(base, column, width):
        rows = arr[pl.ds(base, 4), :, pl.ds(column, width)].reshape(4 * BROWS, width)
        return jnp.dot(lhs[base // 4], rows, preferred_element_type=jnp.float32)

    def add_own(base):
        base = pl.multiple_of(base, 4)
        proj[:, :QC] += multiply(base, 0, QC)
        proj[:, pl.ds(own_col, HD)] += multiply(base, own_col, HD)

    def add_other(base):
        base = pl.multiple_of(base, 4)
        proj[:, pl.ds(other_col, HD)] += multiply(base, other_col, HD)

    def unit_of(event):
        kind, item = event[0], event[1]
        unit = ITEMS[item][0]
        if kind in ("entry", "pair"):
            return (kind, unit)
        way = event[2] if kind == "late" else kind
        side = 1 if kind == "late" else event[2]
        far = way in ("up2", "down2")
        return ("far" if far else way, side, unit)

    missing = {}
    for event in EVENTS:
        missing.setdefault(unit_of(event), set()).add(event)
    base_of = {}
    ready = []
    for name, members in missing.items():
        some = next(event for event in EVENTS if event in members)
        kind = some[0]
        if kind == "entry":
            base_of[name] = unit_base(name[1], z, p)
        elif kind == "pair":
            base_of[name] = unit_base(name[1], z, 1 - p)
        else:
            z_of = {"up1": up_z, "down1": down_z, "far": far_z}[name[0]]
            base_of[name] = unit_base(name[2], z_of, (p + name[1]) % 2)
    members_of = {name: sorted(events, key=PLACE.get) for name, events in missing.items()}
    waiting_other = []
    prepared = False
    cache_rows = iter(range(ROWS))
    for step, event in enumerate(EVENTS):
        wait_for(event)
        forward(event)
        share(event)
        if event == ("entry", 4):
            for unit in (4, 5, 6, 7):
                send_unit(unit)
        name = unit_of(event)
        missing[name].remove(event)
        if not missing[name]:
            ready.append(name)
        if step == 8:
            prepare()
            prepared = True
        if step >= 12:
            row = next(cache_rows, None)
            if row is not None:
                send_cache(row)
        if prepared:
            for name in ready:
                add_own(base_of[name])
                waiting_other.append(name)
            ready = []
            while len(waiting_other) > 6:
                name = waiting_other.pop(0)
                for member in members_of[name]:
                    shared_wait(member)
                add_other(base_of[name])
    for name in waiting_other:
        for member in members_of[name]:
            shared_wait(member)
        add_other(base_of[name])

    for link, slots in sent.items():
        wait_bytes(slots, link_sem.at[link_index[link]])
    wait_bytes(30, stage_sem.at[0])
    everything = arr.at[:, :, pl.ds(QC, HD)]
    pltpu.make_async_copy(everything, everything, kv_send.at[0]).wait()
    pltpu.make_async_copy(cache, cache, cache_send.at[0]).wait()
    pltpu.make_async_copy(cache, cache, cache_recv.at[0]).wait()


def attend_kernel(
    slot_ref,
    len_ref,
    arr,
    proj,
    cos_ref,
    sin_ref,
    cache,
    cache_other,
    served,
    context,
    kv,
    queries,
    scores,
    probs,
    outs,
    kv_sem,
    served_sem,
):
    c = lax.axis_index("tensor") % 2
    groups = 4
    per = ROWS // groups

    def load(group, half):
        rows = pl.ds(group * per, per)
        return pltpu.make_async_copy(
            (cache, cache_other)[half].at[rows], kv.at[rows, pl.ds(half * HALF, HALF)], kv_sem.at[group, half]
        )

    for group in range(groups):
        for half in range(2):
            load(group, half).start()

    def install(b):
        pltpu.make_async_copy(
            arr.at[slot_ref[b]], served.at[0, pl.ds(pl.multiple_of(b * BROWS, BROWS), BROWS)], served_sem.at[0]
        ).start()

    def rotate(block):
        return (block * cos_ref[...] + pltpu.roll(block, HD // 2, 1) * sin_ref[...]).astype(jnp.bfloat16)

    for head in range(HEADS):
        turned = rotate(proj[:, pl.ds(head * HD, HD)]).astype(jnp.float32)
        for s in range(STEPS):
            queries[:, s * HEADS + head, :] = turned[s * ROWS : (s + 1) * ROWS]
    keys_new = rotate(proj[:, pl.ds(QC, HD)]).astype(jnp.float32).reshape(STEPS, ROWS, 1, HD)
    values_new = proj[:, pl.ds(QC + HD, HD)].astype(jnp.bfloat16).astype(jnp.float32)
    values_new = values_new.reshape(STEPS, ROWS, 1, HD)

    scale_factor = HD ** (-0.5)
    column = lax.broadcasted_iota(jnp.int32, (1, LEN), 1)
    position = jnp.where(column < HALF, column + c * HALF, column - c * HALF)
    dims = (((1,), (1,)), ((), ()))

    for group in range(groups):
        for half in range(2):
            load(group, half).wait()

        def score(i, carry):
            b = group * per + i
            for k in range(NB // ROWS):
                install(b * (NB // ROWS) + k)
            found = lax.dot_general(
                queries[b].astype(jnp.bfloat16), kv[b, :, :HD], dims, preferred_element_type=jnp.float32
            )
            scores[b] = jnp.where(position < len_ref[b], found * scale_factor, masked_score)
            return carry

        lax.fori_loop(0, per, score, 0, unroll=2)

    query = queries[...]
    fresh = [jnp.sum(query * keys_new[s], axis=-1, keepdims=True) * scale_factor for s in range(STEPS)]
    step = lax.broadcasted_iota(jnp.int32, (ROWS, STEPS * HEADS, 1), 1) // HEADS
    fresh[1] = jnp.where(step >= 1, fresh[1], masked_score)
    found = scores[...]
    peaks = jnp.maximum(jnp.max(found, axis=-1, keepdims=True), jnp.maximum(fresh[0], fresh[1]))
    weights = jnp.exp(found - peaks).astype(jnp.bfloat16)
    probs[...] = weights
    total = jnp.sum(weights.astype(jnp.float32), axis=-1, keepdims=True)
    fresh = [jnp.exp(one - peaks).astype(jnp.bfloat16).astype(jnp.float32) for one in fresh]
    total = total + fresh[0] + fresh[1]
    extra = fresh[0] * values_new[0] + fresh[1] * values_new[1]

    def gather(b, carry):
        outs[b] = jnp.dot(probs[b], kv[b, :, HD:], preferred_element_type=jnp.float32)
        return carry

    lax.fori_loop(0, ROWS, gather, 0, unroll=4)
    outs[...] = (outs[...] + extra) / total
    for head in range(HEADS):
        for s in range(STEPS):
            context[pl.ds(s * ROWS, ROWS), pl.ds(head * HD, HD)] = outs[:, s * HEADS + head, :].astype(jnp.bfloat16)
    pltpu.make_async_copy(served, served, served_sem.at[0]).wait()


def on_device(hidden_in, norm_gain, qkv_buckets, bucket_slot, kv_cache, cache_len):
    any_space = pl.BlockSpec(memory_space=pl.ANY)
    vmem = pl.BlockSpec(memory_space=pltpu.VMEM)
    smem = pl.BlockSpec(memory_space=pltpu.SMEM)
    freqs = rope_base ** (-2.0 * jnp.arange(HD // 2, dtype=jnp.float32) / HD)
    freqs = jnp.concatenate([freqs, freqs]).reshape(1, HD)
    dma = pltpu.SemaphoreType.DMA
    arr, proj, cosine, sine, cache_other = pl.pallas_call(
        gather_kernel,
        out_shape=[
            pltpu.VMEM((NB, BROWS, COLS), jnp.bfloat16),
            pltpu.VMEM((M, COLS), jnp.float32),
            pltpu.VMEM((M, HD), jnp.float32),
            pltpu.VMEM((M, HD), jnp.float32),
            jax.ShapeDtypeStruct(kv_cache.shape, kv_cache.dtype),
        ],
        in_specs=[any_space] * 5 + [vmem, smem],
        out_specs=[vmem] * 4 + [any_space],
        scratch_shapes=[
            pltpu.VMEM((M, D), jnp.bfloat16),
            pltpu.VMEM((1, D), jnp.float32),
            pltpu.VMEM((1, NB), jnp.int32),
            pltpu.VMEM((1, NB), jnp.int32),
            pltpu.SMEM((1, NB), jnp.int32),
            pltpu.VMEM((NB, BROWS, M), jnp.bfloat16),
            pltpu.VMEM((NB // 4, M, 4 * BROWS), jnp.bfloat16),
            dma((1,)),
            dma((4,)),
            dma((2,)),
            dma((len(EVENTS),)),
            dma((16,)),
            dma((3,)),
            dma((1,)),
            dma((1,)),
            dma((len(EVENTS),)),
            dma((1,)),
            dma((1,)),
        ],
        compiler_params=pltpu.CompilerParams(
            collective_id=0, has_side_effects=True, vmem_limit_bytes=10 * 2**20
        ),
        name="gather_and_project",
    )(
        hidden_in.reshape(M, D),
        norm_gain.reshape(1, D),
        qkv_buckets,
        bucket_slot.reshape(1, NB),
        kv_cache,
        freqs,
        cache_len,
    )
    served, context = pl.pallas_call(
        attend_kernel,
        out_shape=[
            jax.ShapeDtypeStruct((1, D, COLS), jnp.bfloat16),
            jax.ShapeDtypeStruct((M, QC), jnp.bfloat16),
        ],
        in_specs=[smem, smem] + [vmem] * 4 + [any_space] * 2,
        out_specs=[any_space, vmem],
        scratch_shapes=[
            pltpu.VMEM((ROWS, LEN, 2 * HD), jnp.bfloat16),
            pltpu.VMEM((ROWS, STEPS * HEADS, HD), jnp.float32),
            pltpu.VMEM((ROWS, STEPS * HEADS, LEN), jnp.float32),
            pltpu.VMEM((ROWS, STEPS * HEADS, LEN), jnp.bfloat16),
            pltpu.VMEM((ROWS, STEPS * HEADS, HD), jnp.float32),
            dma((4, 2)),
            dma((1,)),
        ],
        compiler_params=pltpu.CompilerParams(vmem_limit_bytes=24 * 2**20),
        name="attend_and_install",
    )(bucket_slot, cache_len, arr, proj, cosine, sine, kv_cache, cache_other)
    return context.reshape(STEPS, ROWS, QC), served


def solution(mesh):
    in_specs = (
        P(None, "replica", None),
        P(),
        P(("replica", "tensor"), None, None),
        P(),
        P("replica", "tensor", None),
        P("replica"),
    )
    out_specs = (P(None, "replica", "tensor"), P("tensor", None, None))
    return jax.shard_map(
        on_device, mesh=mesh, in_specs=in_specs, out_specs=out_specs, check_vma=False
    )
```

time: 240 us -> 110 us (0.46)
  the two profiles are of different devices: /device:TPU:67 before, /device:TPU:1 now
where the time goes in v1:
time: 110 us
  Pallas kernels  91.8 us (83%)
  local copies, waits for them, and re-layouts  17.2 us (16%)
    pallas_call x1, Pallas kernels, on_device(): pl.pallas_call(gather_kernel, out_shape=[pltpu.VMEM((NB, BROWS, COLS), jn...  84.1 us
    unnamed x22, local copies, waits for them, and re-layouts  17.2 us
    pallas_call x1, Pallas kernels, on_device(): pl.pallas_call(attend_kernel, out_shape=[jax.ShapeDtypeStruct((1, D, COLS...  7.68 us

profile of v1, /device:TPU:1, one launch (start us, length us, event | category | flops | bytes accessed | tf_op | source)
XLA Modules:
  0.0 109.8 jit_solution(8160013473875518996)
XLA Ops:
  0.6 0.0 copy-start.10
  0.6 0.0 copy-start.8
  0.7 0.1 maximum_bitcast_fusion.freq_ref
  0.7 0.0 copy-start
  0.7 3.4 %copy-done = bf16[16,1024,256]{2,1,0:T(8,128)(2,1)S(1)} copy-done((bf16[16,1024,256]{2,1,0:T(8,128)(2,1)S(1)}, bf16[16,1024,256]{2,1,0:T(8,128)(2,1)}, u32[]{:S(2)}) %copy-start) | copy-done | bytes 8388632
  4.1 0.0 copy-start.4
  4.1 1.3 %copy-done.4 = bf16[2,32,10240]{2,1,0:T(8,128)(2,1)S(1)} copy-done((bf16[2,32,10240]{2,1,0:T(8,128)(2,1)S(1)}, bf16[2,32,10240]{2,1,0:T(8,128)(2,1)}, u32[]{:S(2)}) %copy-start.4) | copy-done | bytes 1310744
  5.4 0.0 copy-start.5
  5.4 1.0 copy-done.5
  6.5 0.0 copy-start.6
  6.5 0.8 copy-done.6
  7.2 0.0 copy-start.7
  7.2 0.7 copy-done.7
  7.9 0.0 copy-start.9
  7.9 0.7 copy-done.9
  8.6 0.0 copy-start.1
  8.6 84.1 %gather_and_project.1 = (bf16[256,32,768]{2,1,0:T(8,128)(2,1)S(1)}, f32[32,768]{1,0:T(8,128)S(1)}, f32[32,128]{1,0:T(8,128)S(1)}, f32[32,128]{1,0:T(8,128)S(1)}, bf16[16,1024,256]{2,1,0:T(8,128)(2,1)S(1)}) custom-call(bf16[32,8192]{1,0:T(8,128)(2,1)S(1)} %bitcast.6, f32[1,8192]{1,0:T(1,128)S(1)} %bitcast.7, bf16[2,32,10240]{2,1,0:T(8,128)(2,1)S(1)} %copy-done.4, ...), custom_call_target="tpu_custom_call" | custom-call | tf_op jit(solution)/shard_map/gather_and_project/pallas_call | solution.py:531
  92.7 0.0 copy-start.2
  92.7 4.8 %copy-done.2 = bf16[256,32,768]{2,1,0:T(8,128)(2,1)} copy-done((bf16[256,32,768]{2,1,0:T(8,128)(2,1)}, bf16[256,32,768]{2,1,0:T(8,128)(2,1)S(1)}, u32[]{:S(2)}) %copy-start.2) | copy-done | bytes 12582936
  97.5 0.0 copy-done.10
  97.5 0.0 copy-done.8
  97.5 0.0 copy-done.1
  97.5 0.0 copy-start.3
  97.5 4.6 %copy-done.3 = bf16[256,32,768]{2,1,0:T(8,128)(2,1)S(1)} copy-done((bf16[256,32,768]{2,1,0:T(8,128)(2,1)S(1)}, bf16[256,32,768]{2,1,0:T(8,128)(2,1)}, u32[]{:S(2)}) %copy-start.3) | copy-done | bytes 12582936
  102.1 7.7 %attend_and_install.1 = (bf16[1,8192,768]{2,1,0:T(8,128)(2,1)}, bf16[32,512]{1,0:T(8,128)(2,1)}) custom-call(s32[256]{0:T(256)S(1)} %copy-done.8, s32[16]{0:T(128)S(1)} %copy-done.10, bf16[256,32,768]{2,1,0:T(8,128)(2,1)S(1)} %copy-done.3, f32[32,768]{1,0:T(8,128)S(1)} %get-tuple-element.10.proj, f32[32,128]{1,0:T(8,128)S(1)} %get-tuple-element.11.cos_ref, ...), custom_call_target="tpu_custom_call" | custom-call | tf_op jit(solution)/shard_map/attend_and_install/pallas_call | solution.py:575
  (1 shorter events, 0.0 us)
Async XLA Ops:
  0.6 96.9 %copy-start.10 = (s32[16]{0:T(128)S(1)}, s32[16]{0:T(128)}, u32[]{:S(2)}) copy-start(s32[16]{0:T(128)} %len_ref.3) | copy-start | bytes 196
  0.6 96.9 %copy-start.8 = (s32[256]{0:T(256)S(1)}, s32[256]{0:T(256)}, u32[]{:S(2)}) copy-start(s32[256]{0:T(256)} %slot_ref.1) | copy-start | bytes 3076
  0.7 3.4 %copy-start = (bf16[16,1024,256]{2,1,0:T(8,128)(2,1)S(1)}, bf16[16,1024,256]{2,1,0:T(8,128)(2,1)}, u32[]{:S(2)}) copy-start(bf16[16,1024,256]{2,1,0:T(8,128)(2,1)} %cache.3) | copy-start | bytes 25165828
  4.1 1.3 %copy-start.4 = (bf16[2,32,10240]{2,1,0:T(8,128)(2,1)S(1)}, bf16[2,32,10240]{2,1,0:T(8,128)(2,1)}, u32[]{:S(2)}) copy-start(bf16[2,32,10240]{2,1,0:T(8,128)(2,1)} %buckets.1) | copy-start | bytes 3932164
  5.4 1.0 copy-start.5
  6.5 0.8 copy-start.6
  7.2 0.7 copy-start.7
  7.9 0.7 copy-start.9
  8.6 88.9 %copy-start.1 = (bf16[16,1024,256]{2,1,0:T(8,128)(2,1)S(1)}, bf16[16,1024,256]{2,1,0:T(8,128)(2,1)}, u32[]{:S(2)}) copy-start(bf16[16,1024,256]{2,1,0:T(8,128)(2,1)} %cache.3) | copy-start | bytes 25165828
  92.7 4.8 %copy-start.2 = (bf16[256,32,768]{2,1,0:T(8,128)(2,1)}, bf16[256,32,768]{2,1,0:T(8,128)(2,1)S(1)}, u32[]{:S(2)}) copy-start(bf16[256,32,768]{2,1,0:T(8,128)(2,1)S(1)} %get-tuple-element.9.arr) | copy-start | bytes 37748740
  97.5 4.6 %copy-start.3 = (bf16[256,32,768]{2,1,0:T(8,128)(2,1)S(1)}, bf16[256,32,768]{2,1,0:T(8,128)(2,1)}, u32[]{:S(2)}) copy-start(bf16[256,32,768]{2,1,0:T(8,128)(2,1)} %copy-done.2) | copy-start | bytes 37748740

commit v2 on v1

--- a/solution.py
+++ b/solution.py
@@ -41,7 +41,7 @@
 
 def event_order():
     per_slot, hop = 0.87, 0.8
-    entry = (0.8, 1.2, 4.0, 4.0, 4.5, 7.5, 8.5, 13.0, 14.0)
+    entry = (0.7, 0.7, 5.0, 5.0, 5.5, 10.0, 11.0, 15.0, 16.0)
     links = ("pair", "up", "down")
     free = dict.fromkeys(links, 0.0)
     queue = {link: [] for link in links}
@@ -94,24 +94,27 @@
     slot_hbm,
     cache,
     freq_ref,
-    len_ref,
+    len_hbm,
     arr,
     proj,
     cos_ref,
     sin_ref,
-    cache_other,
+    kv,
     hid,
     gain,
     slot_row,
     inv_row,
     inv,
+    len_ref,
+    factor,
     turned,
     lhs,
-    local_sem,
     prep_sem,
     own_sem,
     recv_sem,
+    recv_kv_sem,
     entry_sem,
+    entry_kv_sem,
     link_sem,
     stage_sem,
     kv_send,
@@ -124,11 +127,13 @@
     z, p = r // 2, r % 2
     x, h, c = t // 4, (t // 2) % 2, t % 2
     other_core = (r, x * 4 + h * 2 + (1 - c))
-    target = {
-        "pair": (z * 2 + (1 - p), t),
-        "up": (((z + 1) % 4) * 2 + p, t),
-        "down": (((z + 3) % 4) * 2 + p, t),
+    next_replica = {
+        "pair": z * 2 + (1 - p),
+        "up": ((z + 1) % 4) * 2 + p,
+        "down": ((z + 3) % 4) * 2 + p,
     }
+    target = {link: (replica, t) for link, replica in next_replica.items()}
+    across = {link: (replica, other_core[1]) for link, replica in next_replica.items()}
     own_col = pl.multiple_of(QC + HD * c, HD)
     other_col = pl.multiple_of(QC + HD * (1 - c), HD)
 
@@ -136,6 +141,7 @@
         pltpu.make_async_copy(hid_hbm, hid, prep_sem.at[0]),
         pltpu.make_async_copy(gain_hbm, gain, prep_sem.at[1]),
         pltpu.make_async_copy(slot_hbm, slot_row, prep_sem.at[2]),
+        pltpu.make_async_copy(len_hbm, len_ref, prep_sem.at[3]),
     ]
     for copy in prep:
         copy.start()
@@ -144,59 +150,65 @@
         return (z * 2 + (p + dh) % 2, ((x + dx) % 4) * 4 + ((h + dh) % 2) * 2 + core)
 
     barrier = pltpu.get_barrier_semaphore()
-    peers = [other_core] + list(target.values())
+    peers = [other_core] + list(target.values()) + list(across.values())
     peers += [chip(dx, dh, core) for dx, dh in UNITS[1:] for core in range(2)]
     for peer in peers:
         pl.semaphore_signal(barrier, inc=1, device_id=peer, device_id_type=MESH)
     pl.semaphore_wait(barrier, len(peers))
 
     mine = (r * N_TENSOR + t) * 2
+    sent = {"pair": 0, "up": 0, "down": 0}
+    link_index = {"pair": 0, "up": 1, "down": 2}
 
     def parts(base, slots):
         rows = pl.ds(base, slots)
-        return arr.at[rows, :, pl.ds(0, QC)], arr.at[rows, :, pl.ds(own_col, HD)]
+        return arr.at[rows, :, pl.ds(own_col, HD)], arr.at[rows, :, pl.ds(0, QC)]
 
     def bucket_parts(x_to, h_to, core):
         group = x_to * 2 + h_to
         query = pl.multiple_of((group * 2 + core) * QC, QC)
         key = pl.multiple_of(QH * HD + core * (KVH * HD) + group * HD, HD)
-        return buckets.at[:, :, pl.ds(query, QC)], buckets.at[:, :, pl.ds(key, HD)]
+        return buckets.at[:, :, pl.ds(key, HD)], buckets.at[:, :, pl.ds(query, QC)]
+
+    def own_columns(core):
+        return pl.ds(pl.multiple_of(QC + HD * core, HD), HD), pl.ds(0, QC)
+
+    def send_mine(x_to, h_to, core, dst, send_sem, recv_sems):
+        for src, cols, recv in zip(bucket_parts(x_to, h_to, core), own_columns(core), recv_sems):
+            pltpu.make_async_remote_copy(
+                src_ref=src,
+                dst_ref=arr.at[pl.ds(mine, 2), :, cols],
+                send_sem=send_sem,
+                recv_sem=recv,
+                device_id=dst,
+                device_id_type=MESH,
+            ).start()
 
     def send_unit(unit):
         dx, dh = UNITS[unit]
         x_to, h_to, p_to = (x + 4 - dx) % 4, (h + dh) % 2, (p + dh) % 2
+        sems = (entry_kv_sem.at[2 * unit + c], entry_sem.at[2 * unit + c])
         for core in range(2):
             dst = (z * 2 + p_to, x_to * 4 + h_to * 2 + core)
-            source = bucket_parts(x_to, h_to, core)
-            cols = (pl.ds(0, QC), pl.ds(QC + HD * core, HD))
-            for src, col in zip(source, cols):
-                pltpu.make_async_remote_copy(
-                    src_ref=src,
-                    dst_ref=arr.at[pl.ds(mine, 2), :, col],
-                    send_sem=stage_sem.at[0],
-                    recv_sem=entry_sem.at[2 * unit + c],
-                    device_id=dst,
-                    device_id_type=MESH,
-                ).start()
-
-    def wait_bytes(slots, sem):
-        ref = arr.at[pl.ds(0, slots), :, pl.ds(0, OWN)]
+            send_mine(x_to, h_to, core, dst, stage_sem.at[0], sems)
+
+    def wait_bytes(slots, sem, width=OWN):
+        ref = arr.at[pl.ds(0, slots), :, pl.ds(0, width)]
         pltpu.make_async_copy(ref, ref, sem).wait()
 
+    for item, core in ((0, c), (1, 1 - c)):
+        for link, arrival, slots in forwards(("entry", item)):
+            place_of = PLACE[arrival]
+            dst = (target, across)[item][link]
+            sems = (recv_kv_sem.at[place_of], recv_sem.at[place_of])
+            send_mine(x, h, core, dst, link_sem.at[link_index[link]], sems)
+            sent[link] += slots
     own_copies = []
     for src, dst in zip(bucket_parts(x, h, c), parts(mine, 2)):
         copy = pltpu.make_async_copy(src, dst, own_sem.at[len(own_copies)])
         copy.start()
         own_copies.append(copy)
-    for src, col in zip(bucket_parts(x, h, 1 - c), (pl.ds(0, QC), pl.ds(other_col, HD))):
-        pltpu.make_async_remote_copy(
-            src_ref=src,
-            dst_ref=arr.at[pl.ds(mine, 2), :, col],
-            send_sem=stage_sem.at[0],
-            recv_sem=entry_sem.at[0],
-            device_id=other_core,
-            device_id_type=MESH,
-        ).start()
+    send_mine(x, h, 1 - c, other_core, stage_sem.at[0], (entry_kv_sem.at[0], entry_sem.at[0]))
     for unit in (1, 2, 3):
         send_unit(unit)
 
@@ -233,38 +245,38 @@
             base = base + first
         return base, slots
 
-    def wait_for(event):
+    def wait_for(event, part):
+        width = (HD, QC)[part]
         if event == ("entry", 0):
-            for copy in own_copies:
-                copy.wait()
+            own_copies[part].wait()
         elif event == ("entry", 1):
-            wait_bytes(2, entry_sem.at[0])
+            wait_bytes(2, (entry_kv_sem, entry_sem)[part].at[0], width)
         elif event[0] == "entry":
             unit = ITEMS[event[1]][0]
             for core in range(2):
-                wait_bytes(2, entry_sem.at[2 * unit + core])
+                wait_bytes(2, (entry_kv_sem, entry_sem)[part].at[2 * unit + core], width)
         else:
-            wait_bytes(place(event)[1], recv_sem.at[PLACE[event]])
-
-    sent = {"pair": 0, "up": 0, "down": 0}
-    link_index = {"pair": 0, "up": 1, "down": 2}
-
-    def forward(event):
+            wait_bytes(place(event)[1], (recv_kv_sem, recv_sem)[part].at[PLACE[event]], width)
+
+    def forward(event, part):
+        if event in (("entry", 0), ("entry", 1)):
+            return
         base, _ = place(event)
         for link, arrival, slots in forwards(event):
             start = base
             if arrival[0] == "down2":
                 start = base + slots
-            for ref in parts(start, slots):
-                pltpu.make_async_remote_copy(
-                    src_ref=ref,
-                    dst_ref=ref,
-                    send_sem=link_sem.at[link_index[link]],
-                    recv_sem=recv_sem.at[PLACE[arrival]],
-                    device_id=target[link],
-                    device_id_type=MESH,
-                ).start()
-            sent[link] += slots
+            ref = parts(start, slots)[part]
+            pltpu.make_async_remote_copy(
+                src_ref=ref,
+                dst_ref=ref,
+                send_sem=link_sem.at[link_index[link]],
+                recv_sem=(recv_kv_sem, recv_sem)[part].at[PLACE[arrival]],
+                device_id=target[link],
+                device_id_type=MESH,
+            ).start()
+            if part == 1:
+                sent[link] += slots
 
     def share(event):
         base, slots = place(event)
@@ -283,17 +295,40 @@
         ref = arr.at[pl.ds(0, slots), :, pl.ds(QC, HD)]
         pltpu.make_async_copy(ref, ref, kv_recv.at[PLACE[event]]).wait()
 
+    own_half = pl.ds(pl.multiple_of(c * HALF, HALF), HALF)
+
     def send_cache(row):
+        pltpu.make_async_copy(cache.at[row], kv.at[row, own_half], cache_send.at[1]).start()
         pltpu.make_async_remote_copy(
-            src_ref=cache.at[pl.ds(row, 1)],
-            dst_ref=cache_other.at[pl.ds(row, 1)],
+            src_ref=cache.at[row],
+            dst_ref=kv.at[row, own_half],
             send_sem=cache_send.at[0],
             recv_sem=cache_recv.at[0],
             device_id=other_core,
             device_id_type=MESH,
         ).start()
 
-    def prepare():
+    def squares(j, total):
+        part = hid[:, pl.ds(pl.multiple_of(j * 512, 512), 512)].astype(jnp.float32)
+        return total + jnp.sum(part * part, axis=-1, keepdims=True)
+
+    def turn(j, carry):
+        cols = pl.ds(pl.multiple_of(j * 128, 128), 128)
+        part = hid[:, cols].astype(jnp.float32) * factor[...] * gain[:, cols]
+        part = part.astype(jnp.bfloat16).astype(jnp.float32)
+        part = jnp.transpose(part).astype(jnp.bfloat16)
+        turned[pl.ds(j * 4, 4)] = part.reshape(4, BROWS, M)
+        return carry
+
+    def pick(j, carry):
+        rows = [turned[inv[0, j * 4 + i]] for i in range(4)]
+        part = jnp.concatenate(rows, axis=0).astype(jnp.float32)
+        lhs[j] = jnp.transpose(part).astype(jnp.bfloat16)
+        return carry
+
+    move = pltpu.make_async_copy(inv_row, inv, prep_sem.at[4])
+
+    def find_slots():
         for copy in prep:
             copy.wait()
         slots = jnp.broadcast_to(slot_row[...], (NB, NB))
@@ -301,35 +336,14 @@
         hit = by_bucket == lax.broadcasted_iota(jnp.int32, (NB, NB), 1)
         bucket = lax.broadcasted_iota(jnp.int32, (NB, NB), 0)
         inv_row[...] = jnp.max(jnp.where(hit, bucket, 0), axis=0, keepdims=True)
-        move = pltpu.make_async_copy(inv_row, inv, prep_sem.at[3])
         move.start()
 
-        def squares(j, total):
-            part = hid[:, pl.ds(pl.multiple_of(j * 512, 512), 512)].astype(jnp.float32)
-            return total + jnp.sum(part * part, axis=-1, keepdims=True)
-
+    def find_factor():
         total = lax.fori_loop(0, D // 512, squares, jnp.zeros((M, 1), jnp.float32))
-        factor = lax.rsqrt(total * (1.0 / D) + norm_eps)
-
-        def turn(j, carry):
-            cols = pl.ds(pl.multiple_of(j * 128, 128), 128)
-            part = hid[:, cols].astype(jnp.float32) * factor * gain[:, cols]
-            part = part.astype(jnp.bfloat16).astype(jnp.float32)
-            part = jnp.transpose(part).astype(jnp.bfloat16)
-            turned[pl.ds(j * 4, 4)] = part.reshape(4, BROWS, M)
-            return carry
-
-        lax.fori_loop(0, D // 128, turn, 0)
+        factor[...] = jnp.broadcast_to(lax.rsqrt(total * (1.0 / D) + norm_eps), (M, HD))
         move.wait()
 
-        def pick(j, carry):
-            rows = [turned[inv[0, j * 4 + i]] for i in range(4)]
-            part = jnp.concatenate(rows, axis=0).astype(jnp.float32)
-            lhs[j] = jnp.transpose(part).astype(jnp.bfloat16)
-            return carry
-
-        lax.fori_loop(0, NB // 4, pick, 0)
-
+    def find_angles():
         row = lax.broadcasted_iota(jnp.int32, (M, HD), 0)
         position = jnp.zeros((M, HD), jnp.int32)
         for b in range(ROWS):
@@ -341,6 +355,14 @@
         sine = jnp.sin(angle)
         sin_ref[...] = jnp.where(lane < HD // 2, -sine, sine)
         proj[...] = jnp.zeros_like(proj)
+
+    slices = 8
+    span = D // 128 // slices
+    prepare = [find_slots, find_factor, find_angles]
+    for body in (turn, pick):
+        for i in range(slices):
+            prepare.append(functools.partial(lax.fori_loop, i * span, (i + 1) * span, body, 0))
+    prepare = iter(prepare)
 
     def multiply(base, column, width):
         rows = arr[pl.ds(base, 4), :, pl.ds(column, width)].reshape(4 * BROWS, width)
@@ -385,9 +407,11 @@
     prepared = False
     cache_rows = iter(range(ROWS))
     for step, event in enumerate(EVENTS):
-        wait_for(event)
-        forward(event)
+        wait_for(event, 0)
+        forward(event, 0)
         share(event)
+        wait_for(event, 1)
+        forward(event, 1)
         if event == ("entry", 4):
             for unit in (4, 5, 6, 7):
                 send_unit(unit)
@@ -395,23 +419,29 @@
         missing[name].remove(event)
         if not missing[name]:
             ready.append(name)
-        if step == 8:
-            prepare()
-            prepared = True
+        if step >= 20 and not prepared:
+            work = next(prepare, None)
+            if work is None:
+                prepared = True
+            else:
+                work()
         if step >= 12:
             row = next(cache_rows, None)
             if row is not None:
                 send_cache(row)
         if prepared:
-            for name in ready:
+            for name in ready[:2]:
                 add_own(base_of[name])
                 waiting_other.append(name)
-            ready = []
-            while len(waiting_other) > 6:
+            ready = ready[2:]
+            while len(waiting_other) > 2:
                 name = waiting_other.pop(0)
                 for member in members_of[name]:
                     shared_wait(member)
                 add_other(base_of[name])
+    for name in ready:
+        add_own(base_of[name])
+        waiting_other.append(name)
     for name in waiting_other:
         for member in members_of[name]:
             shared_wait(member)
@@ -423,6 +453,7 @@
     everything = arr.at[:, :, pl.ds(QC, HD)]
     pltpu.make_async_copy(everything, everything, kv_send.at[0]).wait()
     pltpu.make_async_copy(cache, cache, cache_send.at[0]).wait()
+    pltpu.make_async_copy(cache, cache, cache_send.at[1]).wait()
     pltpu.make_async_copy(cache, cache, cache_recv.at[0]).wait()
 
 
@@ -433,32 +464,15 @@
     proj,
     cos_ref,
     sin_ref,
-    cache,
-    cache_other,
+    kv,
     served,
     context,
-    kv,
     queries,
     scores,
     probs,
     outs,
-    kv_sem,
     served_sem,
 ):
-    c = lax.axis_index("tensor") % 2
-    groups = 4
-    per = ROWS // groups
-
-    def load(group, half):
-        rows = pl.ds(group * per, per)
-        return pltpu.make_async_copy(
-            (cache, cache_other)[half].at[rows], kv.at[rows, pl.ds(half * HALF, HALF)], kv_sem.at[group, half]
-        )
-
-    for group in range(groups):
-        for half in range(2):
-            load(group, half).start()
-
     def install(b):
         pltpu.make_async_copy(
             arr.at[slot_ref[b]], served.at[0, pl.ds(pl.multiple_of(b * BROWS, BROWS), BROWS)], served_sem.at[0]
@@ -476,25 +490,19 @@
     values_new = values_new.reshape(STEPS, ROWS, 1, HD)
 
     scale_factor = HD ** (-0.5)
-    column = lax.broadcasted_iota(jnp.int32, (1, LEN), 1)
-    position = jnp.where(column < HALF, column + c * HALF, column - c * HALF)
+    position = lax.broadcasted_iota(jnp.int32, (1, LEN), 1)
     dims = (((1,), (1,)), ((), ()))
 
-    for group in range(groups):
-        for half in range(2):
-            load(group, half).wait()
-
-        def score(i, carry):
-            b = group * per + i
-            for k in range(NB // ROWS):
-                install(b * (NB // ROWS) + k)
-            found = lax.dot_general(
-                queries[b].astype(jnp.bfloat16), kv[b, :, :HD], dims, preferred_element_type=jnp.float32
-            )
-            scores[b] = jnp.where(position < len_ref[b], found * scale_factor, masked_score)
-            return carry
-
-        lax.fori_loop(0, per, score, 0, unroll=2)
+    def score(b, carry):
+        for k in range(NB // ROWS):
+            install(b * (NB // ROWS) + k)
+        found = lax.dot_general(
+            queries[b].astype(jnp.bfloat16), kv[b, :, :HD], dims, preferred_element_type=jnp.float32
+        )
+        scores[b] = jnp.where(position < len_ref[b], found * scale_factor, masked_score)
+        return carry
+
+    lax.fori_loop(0, ROWS, score, 0, unroll=2)
 
     query = queries[...]
     fresh = [jnp.sum(query * keys_new[s], axis=-1, keepdims=True) * scale_factor for s in range(STEPS)]
@@ -528,35 +536,40 @@
     freqs = rope_base ** (-2.0 * jnp.arange(HD // 2, dtype=jnp.float32) / HD)
     freqs = jnp.concatenate([freqs, freqs]).reshape(1, HD)
     dma = pltpu.SemaphoreType.DMA
-    arr, proj, cosine, sine, cache_other = pl.pallas_call(
+    in_hbm = functools.partial(pltpu.with_memory_space_constraint, memory_space=pltpu.HBM)
+    in_vmem = functools.partial(pltpu.with_memory_space_constraint, memory_space=pltpu.VMEM)
+    arr, proj, cosine, sine, kv = pl.pallas_call(
         gather_kernel,
         out_shape=[
             pltpu.VMEM((NB, BROWS, COLS), jnp.bfloat16),
             pltpu.VMEM((M, COLS), jnp.float32),
             pltpu.VMEM((M, HD), jnp.float32),
             pltpu.VMEM((M, HD), jnp.float32),
-            jax.ShapeDtypeStruct(kv_cache.shape, kv_cache.dtype),
+            pltpu.VMEM((ROWS, LEN, 2 * HD), jnp.bfloat16),
         ],
-        in_specs=[any_space] * 5 + [vmem, smem],
-        out_specs=[vmem] * 4 + [any_space],
+        in_specs=[any_space] * 5 + [vmem, any_space],
+        out_specs=[vmem] * 5,
         scratch_shapes=[
             pltpu.VMEM((M, D), jnp.bfloat16),
             pltpu.VMEM((1, D), jnp.float32),
             pltpu.VMEM((1, NB), jnp.int32),
             pltpu.VMEM((1, NB), jnp.int32),
             pltpu.SMEM((1, NB), jnp.int32),
+            pltpu.SMEM((ROWS,), jnp.int32),
+            pltpu.VMEM((M, HD), jnp.float32),
             pltpu.VMEM((NB, BROWS, M), jnp.bfloat16),
             pltpu.VMEM((NB // 4, M, 4 * BROWS), jnp.bfloat16),
-            dma((1,)),
-            dma((4,)),
+            dma((5,)),
             dma((2,)),
             dma((len(EVENTS),)),
+            dma((len(EVENTS),)),
+            dma((16,)),
             dma((16,)),
             dma((3,)),
             dma((1,)),
             dma((1,)),
             dma((len(EVENTS),)),
-            dma((1,)),
+            dma((2,)),
             dma((1,)),
         ],
         compiler_params=pltpu.CompilerParams(
@@ -564,34 +577,32 @@
         ),
         name="gather_and_project",
     )(
-        hidden_in.reshape(M, D),
-        norm_gain.reshape(1, D),
-        qkv_buckets,
-        bucket_slot.reshape(1, NB),
-        kv_cache,
+        in_hbm(hidden_in.reshape(M, D)),
+        in_hbm(norm_gain.reshape(1, D)),
+        in_hbm(qkv_buckets),
+        in_hbm(bucket_slot.reshape(1, NB)),
+        in_hbm(kv_cache),
         freqs,
-        cache_len,
+        in_hbm(cache_len),
     )
     served, context = pl.pallas_call(
         attend_kernel,
         out_shape=[
-            jax.ShapeDtypeStruct((1, D, COLS), jnp.bfloat16),
+            pltpu.HBM((1, D, COLS), jnp.bfloat16),
             jax.ShapeDtypeStruct((M, QC), jnp.bfloat16),
         ],
-        in_specs=[smem, smem] + [vmem] * 4 + [any_space] * 2,
+        in_specs=[smem, smem] + [vmem] * 5,
         out_specs=[any_space, vmem],
         scratch_shapes=[
-            pltpu.VMEM((ROWS, LEN, 2 * HD), jnp.bfloat16),
             pltpu.VMEM((ROWS, STEPS * HEADS, HD), jnp.float32),
             pltpu.VMEM((ROWS, STEPS * HEADS, LEN), jnp.float32),
             pltpu.VMEM((ROWS, STEPS * HEADS, LEN), jnp.bfloat16),
             pltpu.VMEM((ROWS, STEPS * HEADS, HD), jnp.float32),
-            dma((4, 2)),
             dma((1,)),
         ],
-        compiler_params=pltpu.CompilerParams(vmem_limit_bytes=24 * 2**20),
+        compiler_params=pltpu.CompilerParams(vmem_limit_bytes=12 * 2**20),
         name="attend_and_install",
-    )(bucket_slot, cache_len, arr, proj, cosine, sine, kv_cache, cache_other)
+    )(in_hbm(bucket_slot), in_hbm(cache_len), in_vmem(arr), in_vmem(proj), in_vmem(cosine), in_vmem(sine), in_vmem(kv))
     return context.reshape(STEPS, ROWS, QC), served
 
 

time: 110 us -> 91 us (0.83)
  local copies, waits for them, and re-layouts: 17.2 us -> 0 us
  Pallas kernels: 91.8 us -> 90.1 us
    unnamed x22 -> x0, local copies, waits for them, and re-layouts: 17.2 us -> none
where the time goes in v2:
time: 91 us; the launch traced here: 90.8 us
  Pallas kernels  90.1 us (99%)
    pallas_call x1, Pallas kernels, on_device(): pl.pallas_call(gather_kernel, out_shape=[pltpu.VMEM((NB, BROWS, COLS), jn...  83.4 us
    pallas_call x1, Pallas kernels, on_device(): pl.pallas_call(attend_kernel, out_shape=[pltpu.HBM((1, D, COLS), jnp.bflo...  6.61 us

profile of v2, /device:TPU:1, one launch (start us, length us, event | category | flops | bytes accessed | tf_op | source)
XLA Modules:
  0.0 90.8 jit_solution(7841016349709324244)
XLA Ops:
  0.6 0.1 maximum_bitcast_fusion.freq_ref
  0.7 83.4 %gather_and_project.1 = (bf16[256,32,768]{2,1,0:T(8,128)(2,1)S(1)}, f32[32,768]{1,0:T(8,128)S(1)}, f32[32,128]{1,0:T(8,128)S(1)}, f32[32,128]{1,0:T(8,128)S(1)}, bf16[16,2048,256]{2,1,0:T(8,128)(2,1)S(1)}) custom-call(bf16[32,8192]{1,0:T(8,128)(2,1)} %bitcast.6, f32[1,8192]{1,0:T(1,128)} %bitcast.7, bf16[2,32,10240]{2,1,0:T(8,128)(2,1)} %buckets.1, ...), custom_call_target="tpu_custom_call" | custom-call | tf_op jit(solution)/shard_map/gather_and_project/pallas_call | solution.py:541
  84.2 6.6 %attend_and_install.1 = (bf16[1,8192,768]{2,1,0:T(8,128)(2,1)}, bf16[32,512]{1,0:T(8,128)(2,1)}) custom-call(s32[256]{0:T(256)} %slot_ref.1, s32[16]{0:T(128)} %len_ref.1, bf16[256,32,768]{2,1,0:T(8,128)(2,1)S(1)} %get-tuple-element.9.arr, f32[32,768]{1,0:T(8,128)S(1)} %get-tuple-element.10.proj, f32[32,128]{1,0:T(8,128)S(1)} %get-tuple-element.11.cos_ref, ...), custom_call_target="tpu_custom_call" | custom-call | tf_op jit(solution)/shard_map/attend_and_install/pallas_call | solution.py:588
  (1 shorter events, 0.0 us)

commit v3 on v2

--- a/solution.py
+++ b/solution.py
@@ -41,7 +41,7 @@
 
 def event_order():
     per_slot, hop = 0.87, 0.8
-    entry = (0.7, 0.7, 5.0, 5.0, 5.5, 10.0, 11.0, 15.0, 16.0)
+    entry = (0.7, 0.7, 5.0, 5.0, 5.5, 10.0, 11.0, 15.0, 18.0)
     links = ("pair", "up", "down")
     free = dict.fromkeys(links, 0.0)
     queue = {link: [] for link in links}
@@ -85,6 +85,11 @@
 
 EVENTS = event_order()
 PLACE = {event: i for i, event in enumerate(EVENTS)}
+ARRIVALS = [event for event in EVENTS if event[0] != "entry"]
+RECV = {event: i for i, event in enumerate(ARRIVALS)}
+SPLIT = {event: i for i, event in enumerate(EVENTS[-8:])}
+GROUP_ENDS = (14, 28, 42, 56, 68, 78, 84, 88, len(EVENTS))
+GROUP = {event: sum(PLACE[event] >= end for end in GROUP_ENDS) for event in EVENTS}
 
 
 def gather_kernel(
@@ -112,9 +117,8 @@
     prep_sem,
     own_sem,
     recv_sem,
-    recv_kv_sem,
+    split_sem,
     entry_sem,
-    entry_kv_sem,
     link_sem,
     stage_sem,
     kv_send,
@@ -151,7 +155,7 @@
 
     barrier = pltpu.get_barrier_semaphore()
     peers = [other_core] + list(target.values()) + list(across.values())
-    peers += [chip(dx, dh, core) for dx, dh in UNITS[1:] for core in range(2)]
+    peers += [chip(dx, dh, core) for dx, dh in UNITS[1:4] for core in range(2)]
     for peer in peers:
         pl.semaphore_signal(barrier, inc=1, device_id=peer, device_id_type=MESH)
     pl.semaphore_wait(barrier, len(peers))
@@ -187,7 +191,7 @@
     def send_unit(unit):
         dx, dh = UNITS[unit]
         x_to, h_to, p_to = (x + 4 - dx) % 4, (h + dh) % 2, (p + dh) % 2
-        sems = (entry_kv_sem.at[2 * unit + c], entry_sem.at[2 * unit + c])
+        sems = (entry_sem.at[unit], entry_sem.at[unit])
         for core in range(2):
             dst = (z * 2 + p_to, x_to * 4 + h_to * 2 + core)
             send_mine(x_to, h_to, core, dst, stage_sem.at[0], sems)
@@ -196,11 +200,15 @@
         ref = arr.at[pl.ds(0, slots), :, pl.ds(0, width)]
         pltpu.make_async_copy(ref, ref, sem).wait()
 
+    def recv_of(event, part):
+        if part == 0 and event in SPLIT:
+            return split_sem.at[SPLIT[event]]
+        return recv_sem.at[RECV[event]]
+
     for item, core in ((0, c), (1, 1 - c)):
         for link, arrival, slots in forwards(("entry", item)):
-            place_of = PLACE[arrival]
             dst = (target, across)[item][link]
-            sems = (recv_kv_sem.at[place_of], recv_sem.at[place_of])
+            sems = (recv_of(arrival, 0), recv_of(arrival, 1))
             send_mine(x, h, core, dst, link_sem.at[link_index[link]], sems)
             sent[link] += slots
     own_copies = []
@@ -208,7 +216,7 @@
         copy = pltpu.make_async_copy(src, dst, own_sem.at[len(own_copies)])
         copy.start()
         own_copies.append(copy)
-    send_mine(x, h, 1 - c, other_core, stage_sem.at[0], (entry_kv_sem.at[0], entry_sem.at[0]))
+    send_mine(x, h, 1 - c, other_core, stage_sem.at[0], (entry_sem.at[0], entry_sem.at[0]))
     for unit in (1, 2, 3):
         send_unit(unit)
 
@@ -246,17 +254,20 @@
         return base, slots
 
     def wait_for(event, part):
-        width = (HD, QC)[part]
-        if event == ("entry", 0):
-            own_copies[part].wait()
+        slots = place(event)[1]
+        if event in SPLIT:
+            wait_bytes(slots, recv_of(event, part), (HD, QC)[part])
+        elif part == 0:
+            return
+        elif event == ("entry", 0):
+            for copy in own_copies:
+                copy.wait()
         elif event == ("entry", 1):
-            wait_bytes(2, (entry_kv_sem, entry_sem)[part].at[0], width)
+            wait_bytes(slots, entry_sem.at[0])
         elif event[0] == "entry":
-            unit = ITEMS[event[1]][0]
-            for core in range(2):
-                wait_bytes(2, (entry_kv_sem, entry_sem)[part].at[2 * unit + core], width)
+            wait_bytes(slots, entry_sem.at[ITEMS[event[1]][0]])
         else:
-            wait_bytes(place(event)[1], (recv_kv_sem, recv_sem)[part].at[PLACE[event]], width)
+            wait_bytes(slots, recv_of(event, 1))
 
     def forward(event, part):
         if event in (("entry", 0), ("entry", 1)):
@@ -271,7 +282,7 @@
                 src_ref=ref,
                 dst_ref=ref,
                 send_sem=link_sem.at[link_index[link]],
-                recv_sem=(recv_kv_sem, recv_sem)[part].at[PLACE[arrival]],
+                recv_sem=recv_of(arrival, part),
                 device_id=target[link],
                 device_id_type=MESH,
             ).start()
@@ -285,15 +296,18 @@
             src_ref=ref,
             dst_ref=ref,
             send_sem=kv_send.at[0],
-            recv_sem=kv_recv.at[PLACE[event]],
+            recv_sem=kv_recv.at[GROUP[event]],
             device_id=other_core,
             device_id_type=MESH,
         ).start()
 
-    def shared_wait(event):
-        _, slots = place(event)
-        ref = arr.at[pl.ds(0, slots), :, pl.ds(QC, HD)]
-        pltpu.make_async_copy(ref, ref, kv_recv.at[PLACE[event]]).wait()
+    group_slots = [0] * len(GROUP_ENDS)
+    for event in EVENTS:
+        group_slots[GROUP[event]] += place(event)[1]
+
+    def shared_wait(group):
+        ref = arr.at[pl.ds(0, group_slots[group]), :, pl.ds(QC, HD)]
+        pltpu.make_async_copy(ref, ref, kv_recv.at[group]).wait()
 
     own_half = pl.ds(pl.multiple_of(c * HALF, HALF), HALF)
 
@@ -404,17 +418,26 @@
             base_of[name] = unit_base(name[2], z_of, (p + name[1]) % 2)
     members_of = {name: sorted(events, key=PLACE.get) for name, events in missing.items()}
     waiting_other = []
+    shared = set()
     prepared = False
     cache_rows = iter(range(ROWS))
     for step, event in enumerate(EVENTS):
-        wait_for(event, 0)
-        forward(event, 0)
-        share(event)
-        wait_for(event, 1)
-        forward(event, 1)
+        if event in SPLIT:
+            wait_for(event, 0)
+            forward(event, 0)
+            share(event)
+            wait_for(event, 1)
+            forward(event, 1)
+        else:
+            wait_for(event, 1)
+            forward(event, 1)
+            forward(event, 0)
+            share(event)
         if event == ("entry", 4):
-            for unit in (4, 5, 6, 7):
+            for unit in (4, 5, 6):
                 send_unit(unit)
+        if event == ("entry", 5):
+            send_unit(7)
         name = unit_of(event)
         missing[name].remove(event)
         if not missing[name]:
@@ -434,17 +457,22 @@
                 add_own(base_of[name])
                 waiting_other.append(name)
             ready = ready[2:]
-            while len(waiting_other) > 2:
-                name = waiting_other.pop(0)
-                for member in members_of[name]:
-                    shared_wait(member)
-                add_other(base_of[name])
+            for name in waiting_other[:2]:
+                group = max(GROUP[member] for member in members_of[name])
+                if step >= GROUP_ENDS[group] + 2:
+                    for earlier in range(group + 1):
+                        if earlier not in shared:
+                            shared_wait(earlier)
+                            shared.add(earlier)
+                    add_other(base_of[name])
+                    waiting_other.remove(name)
     for name in ready:
         add_own(base_of[name])
         waiting_other.append(name)
+    for group in range(len(GROUP_ENDS)):
+        if group not in shared:
+            shared_wait(group)
     for name in waiting_other:
-        for member in members_of[name]:
-            shared_wait(member)
         add_other(base_of[name])
 
     for link, slots in sent.items():
@@ -478,6 +506,12 @@
             arr.at[slot_ref[b]], served.at[0, pl.ds(pl.multiple_of(b * BROWS, BROWS), BROWS)], served_sem.at[0]
         ).start()
 
+    def install_all(b, carry):
+        install(b)
+        return carry
+
+    lax.fori_loop(0, NB, install_all, 0, unroll=8)
+
     def rotate(block):
         return (block * cos_ref[...] + pltpu.roll(block, HD // 2, 1) * sin_ref[...]).astype(jnp.bfloat16)
 
@@ -494,15 +528,13 @@
     dims = (((1,), (1,)), ((), ()))
 
     def score(b, carry):
-        for k in range(NB // ROWS):
-            install(b * (NB // ROWS) + k)
         found = lax.dot_general(
             queries[b].astype(jnp.bfloat16), kv[b, :, :HD], dims, preferred_element_type=jnp.float32
         )
         scores[b] = jnp.where(position < len_ref[b], found * scale_factor, masked_score)
         return carry
 
-    lax.fori_loop(0, ROWS, score, 0, unroll=2)
+    lax.fori_loop(0, ROWS, score, 0, unroll=8)
 
     query = queries[...]
     fresh = [jnp.sum(query * keys_new[s], axis=-1, keepdims=True) * scale_factor for s in range(STEPS)]
@@ -521,7 +553,7 @@
         outs[b] = jnp.dot(probs[b], kv[b, :, HD:], preferred_element_type=jnp.float32)
         return carry
 
-    lax.fori_loop(0, ROWS, gather, 0, unroll=4)
+    lax.fori_loop(0, ROWS, gather, 0, unroll=16)
     outs[...] = (outs[...] + extra) / total
     for head in range(HEADS):
         for s in range(STEPS):
@@ -561,14 +593,13 @@
             pltpu.VMEM((NB // 4, M, 4 * BROWS), jnp.bfloat16),
             dma((5,)),
             dma((2,)),
-            dma((len(EVENTS),)),
-            dma((len(EVENTS),)),
-            dma((16,)),
-            dma((16,)),
+            dma((len(ARRIVALS),)),
+            dma((len(SPLIT),)),
+            dma((len(UNITS),)),
             dma((3,)),
             dma((1,)),
             dma((1,)),
-            dma((len(EVENTS),)),
+            dma((len(GROUP_ENDS),)),
             dma((2,)),
             dma((1,)),
         ],

time: 91 us -> 86.4 us (0.949)
  Pallas kernels: 90.1 us -> 85.5 us
    pallas_call x1, Pallas kernels: 83.4 us -> 79.4 us  [on_device(): pl.pallas_call(gather_kernel, out_shape=[pltpu.VMEM((NB, BROWS, COLS), jn...]
where the time goes in v3:
time: 86.4 us; the launch traced here: 86.2 us
  Pallas kernels  85.5 us (99%)
    pallas_call x1, Pallas kernels, on_device(): pl.pallas_call(gather_kernel, out_shape=[pltpu.VMEM((NB, BROWS, COLS), jn...  79.4 us
    pallas_call x1, Pallas kernels, on_device(): pl.pallas_call(attend_kernel, out_shape=[pltpu.HBM((1, D, COLS), jnp.bflo...  6.05 us

profile of v3, /device:TPU:1, one launch (start us, length us, event | category | flops | bytes accessed | tf_op | source)
XLA Modules:
  0.0 86.2 jit_solution(6300778879656715482)
XLA Ops:
  0.6 0.1 maximum_bitcast_fusion.freq_ref
  0.7 79.4 %gather_and_project.1 = (bf16[256,32,768]{2,1,0:T(8,128)(2,1)S(1)}, f32[32,768]{1,0:T(8,128)S(1)}, f32[32,128]{1,0:T(8,128)S(1)}, f32[32,128]{1,0:T(8,128)S(1)}, bf16[16,2048,256]{2,1,0:T(8,128)(2,1)S(1)}) custom-call(bf16[32,8192]{1,0:T(8,128)(2,1)} %bitcast.6, f32[1,8192]{1,0:T(1,128)} %bitcast.7, bf16[2,32,10240]{2,1,0:T(8,128)(2,1)} %buckets.1, ...), custom_call_target="tpu_custom_call" | custom-call | tf_op jit(solution)/shard_map/gather_and_project/pallas_call | solution.py:573
  80.1 6.1 %attend_and_install.1 = (bf16[1,8192,768]{2,1,0:T(8,128)(2,1)}, bf16[32,512]{1,0:T(8,128)(2,1)}) custom-call(s32[256]{0:T(256)} %slot_ref.1, s32[16]{0:T(128)} %len_ref.1, bf16[256,32,768]{2,1,0:T(8,128)(2,1)S(1)} %get-tuple-element.9.arr, f32[32,768]{1,0:T(8,128)S(1)} %get-tuple-element.10.proj, f32[32,128]{1,0:T(8,128)S(1)} %get-tuple-element.11.cos_ref, ...), custom_call_target="tpu_custom_call" | custom-call | tf_op jit(solution)/shard_map/attend_and_install/pallas_call | solution.py:619
  (1 shorter events, 0.0 us)

commit v4 on v3

--- a/solution.py
+++ b/solution.py
@@ -36,11 +36,11 @@
 
 UNITS = ((0, 0), (1, 0), (3, 0), (0, 1), (1, 1), (3, 1), (2, 0), (2, 1))
 ITEMS = ((0, 0, 2), (0, 2, 2)) + tuple((u, 0, 4) for u in range(1, 8))
-PAIR_FIRST = frozenset((0, 2, 4, 5, 7))
+PAIR_FIRST = frozenset((0, 2, 3, 7, 8))
 
 
 def event_order():
-    per_slot, hop = 0.87, 0.8
+    per_slot, hop = 0.87, 2.0
     entry = (0.7, 0.7, 5.0, 5.0, 5.5, 10.0, 11.0, 15.0, 18.0)
     links = ("pair", "up", "down")
     free = dict.fromkeys(links, 0.0)
@@ -87,8 +87,8 @@
 PLACE = {event: i for i, event in enumerate(EVENTS)}
 ARRIVALS = [event for event in EVENTS if event[0] != "entry"]
 RECV = {event: i for i, event in enumerate(ARRIVALS)}
-SPLIT = {event: i for i, event in enumerate(EVENTS[-8:])}
-GROUP_ENDS = (14, 28, 42, 56, 68, 78, 84, 88, len(EVENTS))
+DIRECT = {event: i for i, event in enumerate(EVENTS[-3:])}
+GROUP_ENDS = (14, 28, 42, 56, 68, 78, 82, 85, len(EVENTS) - len(DIRECT))
 GROUP = {event: sum(PLACE[event] >= end for end in GROUP_ENDS) for event in EVENTS}
 
 
@@ -117,7 +117,8 @@
     prep_sem,
     own_sem,
     recv_sem,
-    split_sem,
+    direct_send,
+    direct_recv,
     entry_sem,
     link_sem,
     stage_sem,
@@ -200,15 +201,13 @@
         ref = arr.at[pl.ds(0, slots), :, pl.ds(0, width)]
         pltpu.make_async_copy(ref, ref, sem).wait()
 
-    def recv_of(event, part):
-        if part == 0 and event in SPLIT:
-            return split_sem.at[SPLIT[event]]
+    def recv_of(event):
         return recv_sem.at[RECV[event]]
 
     for item, core in ((0, c), (1, 1 - c)):
         for link, arrival, slots in forwards(("entry", item)):
             dst = (target, across)[item][link]
-            sems = (recv_of(arrival, 0), recv_of(arrival, 1))
+            sems = (recv_of(arrival), recv_of(arrival))
             send_mine(x, h, core, dst, link_sem.at[link_index[link]], sems)
             sent[link] += slots
     own_copies = []
@@ -253,13 +252,9 @@
             base = base + first
         return base, slots
 
-    def wait_for(event, part):
+    def wait_for(event):
         slots = place(event)[1]
-        if event in SPLIT:
-            wait_bytes(slots, recv_of(event, part), (HD, QC)[part])
-        elif part == 0:
-            return
-        elif event == ("entry", 0):
+        if event == ("entry", 0):
             for copy in own_copies:
                 copy.wait()
         elif event == ("entry", 1):
@@ -267,9 +262,9 @@
         elif event[0] == "entry":
             wait_bytes(slots, entry_sem.at[ITEMS[event[1]][0]])
         else:
-            wait_bytes(slots, recv_of(event, 1))
-
-    def forward(event, part):
+            wait_bytes(slots, recv_of(event))
+
+    def forward(event):
         if event in (("entry", 0), ("entry", 1)):
             return
         base, _ = place(event)
@@ -277,17 +272,19 @@
             start = base
             if arrival[0] == "down2":
                 start = base + slots
-            ref = parts(start, slots)[part]
-            pltpu.make_async_remote_copy(
-                src_ref=ref,
-                dst_ref=ref,
-                send_sem=link_sem.at[link_index[link]],
-                recv_sem=recv_of(arrival, part),
-                device_id=target[link],
-                device_id_type=MESH,
-            ).start()
-            if part == 1:
-                sent[link] += slots
+            sends = [(ref, target[link], link_sem.at[link_index[link]], recv_of(arrival)) for ref in parts(start, slots)]
+            if arrival in DIRECT:
+                sends.insert(0, (sends[0][0], across[link], direct_send.at[0], direct_recv.at[DIRECT[arrival]]))
+            for ref, dst, send_sem, recv in sends:
+                pltpu.make_async_remote_copy(
+                    src_ref=ref,
+                    dst_ref=ref,
+                    send_sem=send_sem,
+                    recv_sem=recv,
+                    device_id=dst,
+                    device_id_type=MESH,
+                ).start()
+            sent[link] += slots
 
     def share(event):
         base, slots = place(event)
@@ -303,7 +300,9 @@
 
     group_slots = [0] * len(GROUP_ENDS)
     for event in EVENTS:
-        group_slots[GROUP[event]] += place(event)[1]
+        if event not in DIRECT:
+            group_slots[GROUP[event]] += place(event)[1]
+    direct_slots = [place(event)[1] for event in DIRECT]
 
     def shared_wait(group):
         ref = arr.at[pl.ds(0, group_slots[group]), :, pl.ds(QC, HD)]
@@ -422,16 +421,9 @@
     prepared = False
     cache_rows = iter(range(ROWS))
     for step, event in enumerate(EVENTS):
-        if event in SPLIT:
-            wait_for(event, 0)
-            forward(event, 0)
-            share(event)
-            wait_for(event, 1)
-            forward(event, 1)
-        else:
-            wait_for(event, 1)
-            forward(event, 1)
-            forward(event, 0)
+        wait_for(event)
+        forward(event)
+        if event not in DIRECT:
             share(event)
         if event == ("entry", 4):
             for unit in (4, 5, 6):
@@ -459,7 +451,7 @@
             ready = ready[2:]
             for name in waiting_other[:2]:
                 group = max(GROUP[member] for member in members_of[name])
-                if step >= GROUP_ENDS[group] + 2:
+                if group < len(GROUP_ENDS) and step >= GROUP_ENDS[group] + 2:
                     for earlier in range(group + 1):
                         if earlier not in shared:
                             shared_wait(earlier)
@@ -472,14 +464,16 @@
     for group in range(len(GROUP_ENDS)):
         if group not in shared:
             shared_wait(group)
+    for i, slots in enumerate(direct_slots):
+        wait_bytes(slots, direct_recv.at[i], HD)
     for name in waiting_other:
         add_other(base_of[name])
 
     for link, slots in sent.items():
         wait_bytes(slots, link_sem.at[link_index[link]])
     wait_bytes(30, stage_sem.at[0])
-    everything = arr.at[:, :, pl.ds(QC, HD)]
-    pltpu.make_async_copy(everything, everything, kv_send.at[0]).wait()
+    wait_bytes(sum(group_slots), kv_send.at[0], HD)
+    wait_bytes(sum(direct_slots), direct_send.at[0], HD)
     pltpu.make_async_copy(cache, cache, cache_send.at[0]).wait()
     pltpu.make_async_copy(cache, cache, cache_send.at[1]).wait()
     pltpu.make_async_copy(cache, cache, cache_recv.at[0]).wait()
@@ -594,7 +588,8 @@
             dma((5,)),
             dma((2,)),
             dma((len(ARRIVALS),)),
-            dma((len(SPLIT),)),
+            dma((1,)),
+            dma((len(DIRECT),)),
             dma((len(UNITS),)),
             dma((3,)),
             dma((1,)),

time: 86.4 us -> 83.9 us (0.971)
  Pallas kernels: 85.5 us -> 83 us
    pallas_call x1, Pallas kernels: 79.4 us -> 76.9 us  [on_device(): pl.pallas_call(gather_kernel, out_shape=[pltpu.VMEM((NB, BROWS, COLS), jn...]
where the time goes in v4:
time: 83.9 us; the launch traced here: 83.7 us
  Pallas kernels  83 us (99%)
    pallas_call x1, Pallas kernels, on_device(): pl.pallas_call(gather_kernel, out_shape=[pltpu.VMEM((NB, BROWS, COLS), jn...  76.9 us
    pallas_call x1, Pallas kernels, on_device(): pl.pallas_call(attend_kernel, out_shape=[pltpu.HBM((1, D, COLS), jnp.bflo...  6.05 us

profile of v4, /device:TPU:1, one launch (start us, length us, event | category | flops | bytes accessed | tf_op | source)
XLA Modules:
  0.0 83.7 jit_solution(6320253446296941050)
XLA Ops:
  0.6 0.1 maximum_bitcast_fusion.freq_ref
  0.7 76.9 %gather_and_project.1 = (bf16[256,32,768]{2,1,0:T(8,128)(2,1)S(1)}, f32[32,768]{1,0:T(8,128)S(1)}, f32[32,128]{1,0:T(8,128)S(1)}, f32[32,128]{1,0:T(8,128)S(1)}, bf16[16,2048,256]{2,1,0:T(8,128)(2,1)S(1)}) custom-call(bf16[32,8192]{1,0:T(8,128)(2,1)} %bitcast.6, f32[1,8192]{1,0:T(1,128)} %bitcast.7, bf16[2,32,10240]{2,1,0:T(8,128)(2,1)} %buckets.1, ...), custom_call_target="tpu_custom_call" | custom-call | tf_op jit(solution)/shard_map/gather_and_project/pallas_call | solution.py:567
  77.7 6.1 %attend_and_install.1 = (bf16[1,8192,768]{2,1,0:T(8,128)(2,1)}, bf16[32,512]{1,0:T(8,128)(2,1)}) custom-call(s32[256]{0:T(256)} %slot_ref.1, s32[16]{0:T(128)} %len_ref.1, bf16[256,32,768]{2,1,0:T(8,128)(2,1)S(1)} %get-tuple-element.9.arr, f32[32,768]{1,0:T(8,128)S(1)} %get-tuple-element.10.proj, f32[32,128]{1,0:T(8,128)S(1)} %get-tuple-element.11.cos_ref, ...), custom_call_target="tpu_custom_call" | custom-call | tf_op jit(solution)/shard_map/attend_and_install/pallas_call | solution.py:614
  (1 shorter events, 0.0 us)

commit v5 on v4

--- a/solution.py
+++ b/solution.py
@@ -40,7 +40,7 @@
 
 
 def event_order():
-    per_slot, hop = 0.87, 2.0
+    per_slot, hop = 0.87, 2.5
     entry = (0.7, 0.7, 5.0, 5.0, 5.5, 10.0, 11.0, 15.0, 18.0)
     links = ("pair", "up", "down")
     free = dict.fromkeys(links, 0.0)
@@ -86,7 +86,9 @@
 EVENTS = event_order()
 PLACE = {event: i for i, event in enumerate(EVENTS)}
 ARRIVALS = [event for event in EVENTS if event[0] != "entry"]
-RECV = {event: i for i, event in enumerate(ARRIVALS)}
+BOTH = {"up1": "round1", "down1": "round1", "up2": "round2", "down2": "round2"}
+SHARED = list(dict.fromkeys((BOTH.get(event[0], event[0]),) + event[1:] for event in ARRIVALS))
+RECV = {event: SHARED.index((BOTH.get(event[0], event[0]),) + event[1:]) for event in ARRIVALS}
 DIRECT = {event: i for i, event in enumerate(EVENTS[-3:])}
 GROUP_ENDS = (14, 28, 42, 56, 68, 78, 82, 85, len(EVENTS) - len(DIRECT))
 GROUP = {event: sum(PLACE[event] >= end for end in GROUP_ENDS) for event in EVENTS}
@@ -252,6 +254,8 @@
             base = base + first
         return base, slots
 
+    waited = set()
+
     def wait_for(event):
         slots = place(event)[1]
         if event == ("entry", 0):
@@ -261,8 +265,11 @@
             wait_bytes(slots, entry_sem.at[0])
         elif event[0] == "entry":
             wait_bytes(slots, entry_sem.at[ITEMS[event[1]][0]])
-        else:
+        elif event[0] not in BOTH:
             wait_bytes(slots, recv_of(event))
+        elif RECV[event] not in waited:
+            waited.add(RECV[event])
+            wait_bytes(2 * slots, recv_of(event))
 
     def forward(event):
         if event in (("entry", 0), ("entry", 1)):
@@ -587,7 +594,7 @@
             pltpu.VMEM((NB // 4, M, 4 * BROWS), jnp.bfloat16),
             dma((5,)),
             dma((2,)),
-            dma((len(ARRIVALS),)),
+            dma((len(SHARED),)),
             dma((1,)),
             dma((len(DIRECT),)),
             dma((len(UNITS),)),

time: 83.9 us -> 83.6 us (level)
  no operation moved by 1% of the time
where the time goes in v5:
time: 83.6 us; the launch traced here: 83.5 us
  Pallas kernels  82.7 us (99%)
    pallas_call x1, Pallas kernels, on_device(): pl.pallas_call(gather_kernel, out_shape=[pltpu.VMEM((NB, BROWS, COLS), jn...  76.7 us
    pallas_call x1, Pallas kernels, on_device(): pl.pallas_call(attend_kernel, out_shape=[pltpu.HBM((1, D, COLS), jnp.bflo...  6.05 us

profile of v5, /device:TPU:1, one launch (start us, length us, event | category | flops | bytes accessed | tf_op | source)
XLA Modules:
  0.0 83.5 jit_solution(2948889922963553117)
XLA Ops:
  0.6 0.1 maximum_bitcast_fusion.freq_ref
  0.7 76.7 %gather_and_project.1 = (bf16[256,32,768]{2,1,0:T(8,128)(2,1)S(1)}, f32[32,768]{1,0:T(8,128)S(1)}, f32[32,128]{1,0:T(8,128)S(1)}, f32[32,128]{1,0:T(8,128)S(1)}, bf16[16,2048,256]{2,1,0:T(8,128)(2,1)S(1)}) custom-call(bf16[32,8192]{1,0:T(8,128)(2,1)} %bitcast.6, f32[1,8192]{1,0:T(1,128)} %bitcast.7, bf16[2,32,10240]{2,1,0:T(8,128)(2,1)} %buckets.1, ...), custom_call_target="tpu_custom_call" | custom-call | tf_op jit(solution)/shard_map/gather_and_project/pallas_call | solution.py:574
  77.4 6.1 %attend_and_install.1 = (bf16[1,8192,768]{2,1,0:T(8,128)(2,1)}, bf16[32,512]{1,0:T(8,128)(2,1)}) custom-call(s32[256]{0:T(256)} %slot_ref.1, s32[16]{0:T(128)} %len_ref.1, bf16[256,32,768]{2,1,0:T(8,128)(2,1)S(1)} %get-tuple-element.9.arr, f32[32,768]{1,0:T(8,128)S(1)} %get-tuple-element.10.proj, f32[32,128]{1,0:T(8,128)S(1)} %get-tuple-element.11.cos_ref, ...), custom_call_target="tpu_custom_call" | custom-call | tf_op jit(solution)/shard_map/attend_and_install/pallas_call | solution.py:621
  (1 shorter events, 0.0 us)

commit v6 on v5

--- a/solution.py
+++ b/solution.py
@@ -107,9 +107,10 @@
     cos_ref,
     sin_ref,
     kv,
+    slot_row,
+    len_row,
     hid,
     gain,
-    slot_row,
     inv_row,
     inv,
     len_ref,
@@ -149,6 +150,7 @@
         pltpu.make_async_copy(gain_hbm, gain, prep_sem.at[1]),
         pltpu.make_async_copy(slot_hbm, slot_row, prep_sem.at[2]),
         pltpu.make_async_copy(len_hbm, len_ref, prep_sem.at[3]),
+        pltpu.make_async_copy(len_hbm, len_row, prep_sem.at[5]),
     ]
     for copy in prep:
         copy.start()
@@ -368,7 +370,7 @@
         position = jnp.zeros((M, HD), jnp.int32)
         for b in range(ROWS):
             for s in range(STEPS):
-                position = jnp.where(row == s * ROWS + b, len_ref[b] + s, position)
+                position = jnp.where(row == s * ROWS + b, len_ref[0, b] + s, position)
         angle = position.astype(jnp.float32) * freq_ref[...]
         lane = lax.broadcasted_iota(jnp.int32, (M, HD), 1)
         cos_ref[...] = jnp.cos(angle)
@@ -487,8 +489,8 @@
 
 
 def attend_kernel(
-    slot_ref,
-    len_ref,
+    slot_row,
+    len_row,
     arr,
     proj,
     cos_ref,
@@ -500,11 +502,23 @@
     scores,
     probs,
     outs,
+    slot_ref,
+    len_ref,
+    row_sem,
     served_sem,
 ):
+    rows = [
+        pltpu.make_async_copy(slot_row, slot_ref, row_sem.at[0]),
+        pltpu.make_async_copy(len_row, len_ref, row_sem.at[1]),
+    ]
+    for copy in rows:
+        copy.start()
+    for copy in rows:
+        copy.wait()
+
     def install(b):
         pltpu.make_async_copy(
-            arr.at[slot_ref[b]], served.at[0, pl.ds(pl.multiple_of(b * BROWS, BROWS), BROWS)], served_sem.at[0]
+            arr.at[slot_ref[0, b]], served.at[0, pl.ds(pl.multiple_of(b * BROWS, BROWS), BROWS)], served_sem.at[0]
         ).start()
 
     def install_all(b, carry):
@@ -532,7 +546,7 @@
         found = lax.dot_general(
             queries[b].astype(jnp.bfloat16), kv[b, :, :HD], dims, preferred_element_type=jnp.float32
         )
-        scores[b] = jnp.where(position < len_ref[b], found * scale_factor, masked_score)
+        scores[b] = jnp.where(position < len_ref[0, b], found * scale_factor, masked_score)
         return carry
 
     lax.fori_loop(0, ROWS, score, 0, unroll=8)
@@ -571,7 +585,7 @@
     dma = pltpu.SemaphoreType.DMA
     in_hbm = functools.partial(pltpu.with_memory_space_constraint, memory_space=pltpu.HBM)
     in_vmem = functools.partial(pltpu.with_memory_space_constraint, memory_space=pltpu.VMEM)
-    arr, proj, cosine, sine, kv = pl.pallas_call(
+    arr, proj, cosine, sine, kv, slots, lengths = pl.pallas_call(
         gather_kernel,
         out_shape=[
             pltpu.VMEM((NB, BROWS, COLS), jnp.bfloat16),
@@ -579,20 +593,21 @@
             pltpu.VMEM((M, HD), jnp.float32),
             pltpu.VMEM((M, HD), jnp.float32),
             pltpu.VMEM((ROWS, LEN, 2 * HD), jnp.bfloat16),
+            pltpu.VMEM((1, NB), jnp.int32),
+            pltpu.VMEM((1, ROWS), jnp.int32),
         ],
         in_specs=[any_space] * 5 + [vmem, any_space],
-        out_specs=[vmem] * 5,
+        out_specs=[vmem] * 7,
         scratch_shapes=[
             pltpu.VMEM((M, D), jnp.bfloat16),
             pltpu.VMEM((1, D), jnp.float32),
             pltpu.VMEM((1, NB), jnp.int32),
-            pltpu.VMEM((1, NB), jnp.int32),
             pltpu.SMEM((1, NB), jnp.int32),
-            pltpu.SMEM((ROWS,), jnp.int32),
+            pltpu.SMEM((1, ROWS), jnp.int32),
             pltpu.VMEM((M, HD), jnp.float32),
             pltpu.VMEM((NB, BROWS, M), jnp.bfloat16),
             pltpu.VMEM((NB // 4, M, 4 * BROWS), jnp.bfloat16),
-            dma((5,)),
+            dma((6,)),
             dma((2,)),
             dma((len(SHARED),)),
             dma((1,)),
@@ -616,7 +631,7 @@
         in_hbm(bucket_slot.reshape(1, NB)),
         in_hbm(kv_cache),
         freqs,
-        in_hbm(cache_len),
+        in_hbm(cache_len.reshape(1, ROWS)),
     )
     served, context = pl.pallas_call(
         attend_kernel,
@@ -624,18 +639,21 @@
             pltpu.HBM((1, D, COLS), jnp.bfloat16),
             jax.ShapeDtypeStruct((M, QC), jnp.bfloat16),
         ],
-        in_specs=[smem, smem] + [vmem] * 5,
+        in_specs=[vmem] * 7,
         out_specs=[any_space, vmem],
         scratch_shapes=[
             pltpu.VMEM((ROWS, STEPS * HEADS, HD), jnp.float32),
             pltpu.VMEM((ROWS, STEPS * HEADS, LEN), jnp.float32),
             pltpu.VMEM((ROWS, STEPS * HEADS, LEN), jnp.bfloat16),
             pltpu.VMEM((ROWS, STEPS * HEADS, HD), jnp.float32),
+            pltpu.SMEM((1, NB), jnp.int32),
+            pltpu.SMEM((1, ROWS), jnp.int32),
+            dma((2,)),
             dma((1,)),
         ],
         compiler_params=pltpu.CompilerParams(vmem_limit_bytes=12 * 2**20),
         name="attend_and_install",
-    )(in_hbm(bucket_slot), in_hbm(cache_len), in_vmem(arr), in_vmem(proj), in_vmem(cosine), in_vmem(sine), in_vmem(kv))
+    )(in_vmem(slots), in_vmem(lengths), in_vmem(arr), in_vmem(proj), in_vmem(cosine), in_vmem(sine), in_vmem(kv))
     return context.reshape(STEPS, ROWS, QC), served
 
 

time: 83.6 us -> 83.6 us (level)
  no operation moved by 1% of the time
where the time goes in v6:
time: 83.6 us; the launch traced here: 83.4 us
  Pallas kernels  82.7 us (99%)
    pallas_call x1, Pallas kernels, on_device(): pl.pallas_call(gather_kernel, out_shape=[pltpu.VMEM((NB, BROWS, COLS), jn...  76.7 us
    pallas_call x1, Pallas kernels, on_device(): pl.pallas_call(attend_kernel, out_shape=[pltpu.HBM((1, D, COLS), jnp.bflo...  6.01 us

profile of v6, /device:TPU:1, one launch (start us, length us, event | category | flops | bytes accessed | tf_op | source)
XLA Modules:
  0.0 83.4 jit_solution(14595280943884433392)
XLA Ops:
  0.6 0.1 maximum_bitcast_fusion.freq_ref
  0.7 76.7 %gather_and_project.1 = (bf16[256,32,768]{2,1,0:T(8,128)(2,1)S(1)}, f32[32,768]{1,0:T(8,128)S(1)}, f32[32,128]{1,0:T(8,128)S(1)}, f32[32,128]{1,0:T(8,128)S(1)},...) custom-call(bf16[32,8192]{1,0:T(8,128)(2,1)} %bitcast.7, f32[1,8192]{1,0:T(1,128)} %bitcast.8, ...), custom_call_target="tpu_custom_call" | custom-call | tf_op jit(solution)/shard_map/gather_and_project/pallas_call | solution.py:588
  77.4 6.0 %attend_and_install.1 = (bf16[1,8192,768]{2,1,0:T(8,128)(2,1)}, bf16[32,512]{1,0:T(8,128)(2,1)}) custom-call(s32[1,256]{1,0:T(1,128)S(1)} %get-tuple-element.11.slot_row, s32[1,16]{1,0:T(1,128)S(1)} %get-tuple-element.12.len_row, bf16[256,32,768]{2,1,0:T(8,128)(2,1)S(1)} %get-tuple-element.13.arr, f32[32,768]{1,0:T(8,128)S(1)} %get-tuple-element.14.proj, ...), custom_call_target="tpu_custom_call" | custom-call | tf_op jit(solution)/shard_map/attend_and_install/pallas_call | solution.py:636
  (1 shorter events, 0.0 us)
